TPU v7x, 32 devices: a whole 2x2x4 slice. The times are simulated.
32 devices in a mesh: groups: 2 (over y), blk: 4 (over z), heads: 2 (over x), beam: 2 (over core).
Axes of the slice: x: 2, y: 2, z: 4, core: 2. Of those that a mesh axis runs over, the one named last changes fastest.
Arguments:
- queries: bfloat16 [4, 32, 64, 128], P(('groups', 'beam'), 'blk', 'heads'), parts along dimension 0, may hold values from -110 to 110
- positions: int32 [4, 32], P(('groups', 'beam'), 'blk'), parts along dimension 0, may hold values from 512 to 4096
- row_order: int32 [4, 32], P(('groups', 'beam')), parts along dimension 0, may hold values from 0 to 31, each once within a row
- lengths: int32 [8], P(('groups', 'blk')), parts along dimension 0, may hold values from 128 to 1024
- cache_keys: bfloat16 [8, 4, 1024, 128], P(('groups', 'blk'), 'heads'), parts along dimension 0, may hold values from -4 to 4
- cache_values: bfloat16 [8, 4, 1024, 128], P(('groups', 'blk'), 'heads'), parts along dimension 0, may hold values from -6 to 6
Outputs:
- attended: bfloat16 [4, 32, 64, 128], P(('groups', 'beam'), 'blk', 'heads'), parts along dimension 0
There are 2 independent parts, one for each index of `groups`. A program takes and returns all parts, laid end to end along the dimension named above; each array names one. Nothing has to cross between parts.
Inputs may be any that keep to these rules, and one draw needn't show every extreme that they name: Slots of shard s from lengths[s] on hold no cache entry. row_order[e] is a permutation of 0 to 31.
All inputs are finite; a program needn't handle non-finite values.
Results may differ from a plain program's by a relative error of at most 0.0015.
Values may be sent and summed in bfloat16 or wider, within the bound.
No kernel may reach another device: no remote copies, remote signals or barrier semaphores. Data moves between devices by JAX's collectives and lax.ppermute only.
A program may use at most 64 MiB of HBM per device.

v0:
```python
import jax
import jax.numpy as jnp
from jax import lax
from jax.sharding import PartitionSpec as P

KB = 256


masked_score = -1e30


def entering(value, axis, join, neutral):
    count, mine = (lax.axis_size(axis), lax.axis_index(axis))
    pieces = lax.all_gather(value, axis)
    total = jnp.full_like(value, 0) + jnp.asarray(neutral, value.dtype)

    def turn(position, total):
        longer = join(total, pieces[position])
        return jnp.where(position < mine, longer, total)

    return lax.fori_loop(0, count - 1, turn, total)


def add_counts(earlier, later):
    return earlier + later


def block_partial(
    query_rows, row_positions, key_block, value_block, first_slot, length, offset, scaling
):
    scores = (
        jnp.einsum("rkgd,kjd->rkgj", query_rows, key_block, preferred_element_type=jnp.float32)
        * scaling
    )
    slot_ids = first_slot + lax.iota(jnp.int32, key_block.shape[1])
    visible = (slot_ids < length)[None, :] & ((offset + slot_ids)[None, :] < row_positions[:, None])
    visible = visible[:, None, None, :]
    highest = jnp.max(jnp.where(visible, scores, masked_score), axis=-1)
    weights = jnp.where(visible, jnp.exp(scores - highest[..., None]), 0.0)
    totals = jnp.sum(weights, axis=-1)
    block_out = jnp.einsum(
        "rkgj,kjd->rkgd",
        weights.astype(jnp.bfloat16),
        value_block,
        preferred_element_type=jnp.float32,
    )
    return (block_out, totals, highest)


def combine_parts(running, latest):
    run_out, run_tot, run_top = running
    new_out, new_tot, new_top = latest
    joined = jnp.maximum(run_top, new_top)
    older = jnp.exp(run_top - joined)
    newer = jnp.exp(new_top - joined)
    return (
        run_out * older[..., None] + new_out * newer[..., None],
        run_tot * older + new_tot * newer,
        joined,
    )


def settle(exchanged):
    shard_out, shard_tot, shard_top = exchanged
    highest = jnp.max(shard_top, axis=0)
    factor = jnp.exp(shard_top - highest)
    numerator = jnp.sum(shard_out * factor[..., None], axis=0)
    denominator = jnp.sum(shard_tot * factor, axis=0)
    return numerator / denominator[..., None]


def per_device(queries, positions, row_order, lengths, cache_keys, cache_values):
    offsets = entering(lengths, "blk", add_counts, jnp.zeros_like(lengths))
    length = lengths[0]
    offset = offsets[0]
    key_shard = cache_keys[0]
    value_shard = cache_values[0]
    kv_heads = key_shard.shape[0]
    capacity = key_shard.shape[1]
    head_dim = key_shard.shape[2]
    group = queries.shape[2] // kv_heads
    scaling = float(head_dim) ** (-0.5)
    row_dev = queries.shape[1]
    piece_queries = lax.all_gather(queries, "blk", axis=1, tiled=True)
    piece_positions = lax.all_gather(positions, "blk", axis=1, tiled=True)
    count_rows = piece_queries.shape[1]
    query_rows = piece_queries.reshape(count_rows, kv_heads, group, head_dim)
    row_positions = piece_positions.reshape(count_rows)
    shard_count_rows = query_rows.shape[0]
    running = (
        jnp.zeros((shard_count_rows, kv_heads, group, head_dim), jnp.float32),
        jnp.zeros((shard_count_rows, kv_heads, group), jnp.float32),
        jnp.full((shard_count_rows, kv_heads, group), masked_score, jnp.float32),
    )
    for block in range(capacity // KB):
        first_slot = block * KB
        latest = block_partial(
            query_rows,
            row_positions,
            key_shard[:, first_slot : first_slot + KB],
            value_shard[:, first_slot : first_slot + KB],
            first_slot,
            length,
            offset,
            scaling,
        )
        running = combine_parts(running, latest)
    merged_out, merged_tot, merged_top = tuple((fresh for fresh in running))
    picked = row_order[0]
    merged_out = jnp.take(merged_out, picked, axis=0)
    merged_tot = jnp.take(merged_tot, picked, axis=0)
    merged_top = jnp.take(merged_top, picked, axis=0)
    result = settle(
        (
            lax.all_to_all(merged_out[None], "blk", split_axis=1, concat_axis=0, tiled=True),
            lax.all_to_all(merged_tot[None], "blk", split_axis=1, concat_axis=0, tiled=True),
            lax.all_to_all(merged_top[None], "blk", split_axis=1, concat_axis=0, tiled=True),
        )
    )
    return result.reshape(1, row_dev, kv_heads * group, head_dim).astype(jnp.bfloat16)


def solution(mesh):
    placed = (
        P(("groups", "beam"), "blk", "heads", None),
        P(("groups", "beam"), "blk"),
        P(("groups", "beam"), None),
        P(("groups", "blk")),
        P(("groups", "blk"), "heads", None, None),
        P(("groups", "blk"), "heads", None, None),
    )
    return jax.shard_map(
        per_device,
        mesh=mesh,
        in_specs=placed,
        out_specs=P(("groups", "beam"), "blk", "heads", None),
        check_vma=False,
    )
```

profile of v0, /device:TPU:0, one launch (start us, length us, event | category | flops | bytes accessed | tf_op | source)
XLA Modules:
  0.0 70.2 jit_solution(5707162377590074350)
XLA Ops:
  0.7 0.0 copy-start.5
  0.7 0.6 copy-done.5
  1.3 0.6 dynamic-slice
  2.5 0.7 dynamic-update-slice
  3.1 0.0 copy-start.4
  3.1 0.0 copy-start.3
  3.1 0.7 copy-done.3
  3.8 0.1 bitcast_dynamic-update-slice_fusion
  3.9 9.9 %all-reduce.2 = (s32[4]{0:T(128)S(1)}, s32[32]{0:T(128)S(1)}) all-reduce(s32[4]{0:T(128)S(1)} %dynamic-update-slice, s32[32]{0:T(128)S(1)} %bitcast_dynamic-update-slice_fusion), channel_id=2, replica_groups=mesh['groups'=2,'blk'=4,'heads'=2,'beam'=2] {'blk'}, use_global_device_ids=true, to_apply=%add | all-reduce | flops 36 | bytes 288
  13.8 3.7 %while.13 = (s32[]{:T(128)}, s32[1]{0:T(128)}, s32[]{:T(128)}, s32[4,1]{0,1:T(1,128)S(1)}, s32[]{:T(128)}) while((s32[]{:T(128)}, s32[1]{0:T(128)}, s32[]{:T(128)}, s32[4,1]{0,1:T(1,128)S(1)}, s32[]{:T(128)}) %tuple.58), condition=%wide.region_1.2_spmd, body=%wide.region_0.1_spmd.sunk | while | flops 5 | bytes 115 | solution.py:21
  13.8 0.6 constant_dynamic-slice_fusion.2
  15.0 0.6 constant_dynamic-slice_fusion.2
  16.3 0.6 constant_dynamic-slice_fusion.2
  17.6 0.0 copy-done.4
  17.6 0.0 copy-done.1
  17.6 13.8 %all_gather.15 = bf16[1,32,32,128]{3,2,0,1:T(8,128)(2,1)S(1)} all-gather(bf16[1,8,32,128]{3,2,0,1:T(8,128)(2,1)S(1)} %bitcast.162), channel_id=1, replica_groups=mesh['groups'=2,'blk'=4,'heads'=2,'beam'=2] {'blk'}, dimensions={1}, use_global_device_ids=true | all-gather | bytes 327680 | tf_op jit(solution)/shard_map/all_gather | solution.py:84
  31.4 0.1 copy.107
  31.5 0.1 compare_and_fusion.3
  31.6 0.0 copy-done
  31.6 0.4 select_reduce_fusion
  32.0 0.4 select_reduce_fusion.1
  32.4 0.4 select_reduce_fusion.2
  32.8 0.4 select_reduce_fusion.3
  33.2 0.4 fusion.20
  33.6 0.4 fusion.18
  34.0 0.4 fusion.16
  34.4 0.4 fusion.21
  34.8 0.0 copy-start.2
  34.9 0.1 copy.121
  34.9 0.1 copy.125
  35.0 0.6 gather_fusion.1
  35.6 0.6 gather_fusion.2
  36.2 0.1 select_bitcast_fusion.1
  36.3 0.7 %reshape.392 = f32[4,1,256]{2,1,0:T(1,128)} reshape(f32[32,1,2,16]{3,2,1,0:T(2,128)S(1)} %bitcast.161) | data formatting | bytes 8192
  37.1 3.6 %all-to-all-start.2 = ((f32[4,1,256]{2,1,0:T(1,128)}), f32[4,1,256]{2,1,0:T(1,128)S(1)}, u32[]{:S(2)}, u32[]{:S(2)}) async-start(f32[4,1,256]{2,1,0:T(1,128)} %reshape.392), calls=%async_computation.2 | async-start | bytes 8192 | tf_op jit(solution)/shard_map/all_to_all | solution.py:116
  40.6 0.1 copy.119
  40.7 0.1 copy.116
  40.8 0.1 copy.113
  40.8 0.1 copy.117
  40.9 0.1 copy.114
  41.0 0.1 copy.111
  41.1 0.1 copy.110
  41.1 0.1 copy.108
  41.2 0.0 copy-done.2
  41.2 0.5 fusion.14
  41.7 0.5 fusion.13
  42.2 0.5 fusion.12
  42.6 0.9 %fusion.11 = f32[32,2,16,128]{3,2,0,1:T(8,128)S(1)} fusion(f32[32,2,16,128]{3,2,0,1:T(8,128)S(1)} %fusion.14, f32[32,2,16,128]{3,2,0,1:T(8,128)S(1)} %fusion.13, f32[32,2,16,128]{3,2,0,1:T(8,128)S(1)} %fusion.12, bf16[32,2,16,256]{3,0,2,1:T(8,128)(2,1)S(1)} %get-tuple-element.106, f32[32,2,16]{2,0,1:T(8,128)S(1)} %copy.117, f32[32,2,16]{2,0,1:T(8,128)S(1)} %copy.114, ...), kind=kOutput, calls=%fused_computation.23 | convolution fusion | flops 68157440 | bytes 2916352 | tf_op jit(solution)/shard_map/rkgj,kjd->rkgd/dot_general | solution.py:41
  43.6 0.7 %reshape.390 = f32[4,1,256]{2,1,0:T(1,128)} reshape(f32[32,1,2,16]{3,2,1,0:T(2,128)S(1)} %bitcast.160) | data formatting | bytes 8192
  44.3 0.6 gather_fusion
  44.9 1.3 %all-to-all-done.2 = f32[4,1,256]{2,1,0:T(1,128)S(1)} async-done(((f32[4,1,256]{2,1,0:T(1,128)}), f32[4,1,256]{2,1,0:T(1,128)S(1)}, u32[]{:S(2)}, u32[]{:S(2)}) %all-to-all-start.2) | async-done | bytes 4128 | tf_op jit(solution)/shard_map/all_to_all | solution.py:116
  46.2 3.8 %all-to-all-start.1 = ((f32[4,1,256]{2,1,0:T(1,128)}), f32[4,1,256]{2,1,0:T(1,128)S(1)}, u32[]{:S(2)}, u32[]{:S(2)}) async-start(f32[4,1,256]{2,1,0:T(1,128)} %reshape.390), calls=%async_computation.1 | async-start | bytes 8192 | tf_op jit(solution)/shard_map/all_to_all | solution.py:117
  50.0 0.9 %fusion.23 = f32[1,32,2,16,128]{4,3,2,0,1:T(8,128)} fusion(f32[32,2,16,128]{3,2,1,0:T(8,128)S(1)} %gather_fusion, pred[32]{0:T(512)(128)(4,1)S(1)} %compare_and_fusion.4), kind=kLoop, calls=%fused_computation.44 | loop fusion | flops 131072 | bytes 1048608 | tf_op jit(solution)/shard_map/jit(_take)/select_n | solution.py:110
  50.9 4.7 %all-to-all-done.1 = f32[4,1,256]{2,1,0:T(1,128)S(1)} async-done(((f32[4,1,256]{2,1,0:T(1,128)}), f32[4,1,256]{2,1,0:T(1,128)S(1)}, u32[]{:S(2)}, u32[]{:S(2)}) %all-to-all-start.1) | async-done | bytes 4128 | tf_op jit(solution)/shard_map/all_to_all | solution.py:117
  55.5 3.5 %all-to-all-start = ((f32[1,32,2,16,128]{4,3,2,0,1:T(8,128)}), f32[1,32,2,16,128]{4,3,2,0,1:T(8,128)S(1)}, u32[]{:S(2)}, u32[]{:S(2)}) async-start(f32[1,32,2,16,128]{4,3,2,0,1:T(8,128)} %fusion.23), calls=%async_computation | async-start | bytes 1048576 | tf_op jit(solution)/shard_map/all_to_all | solution.py:115
  59.0 0.5 broadcast.265
  59.5 0.7 reduce
  60.2 0.1 reshape.393
  60.3 0.7 reduce.1
  61.0 0.1 reshape.391
  61.2 0.1 div.18
  61.3 8.0 %all-to-all-done = f32[1,32,2,16,128]{4,3,2,0,1:T(8,128)S(1)} async-done(((f32[1,32,2,16,128]{4,3,2,0,1:T(8,128)}), f32[1,32,2,16,128]{4,3,2,0,1:T(8,128)S(1)}, u32[]{:S(2)}, u32[]{:S(2)}) %all-to-all-start) | async-done | bytes 524320 | tf_op jit(solution)/shard_map/all_to_all | solution.py:115
  69.3 0.2 multiply_reduce_fusion
  69.5 0.7 %divide_convert_fusion = bf16[1,8,32,128]{3,2,1,0:T(8,128)(2,1)} fusion(f32[1,8,32,128]{3,2,1,0:T(8,128)S(1)} %bitcast.156, f32[8,32]{1,0:T(8,128)S(1)} %div.18), kind=kLoop, calls=%fused_computation.58 | loop fusion | flops 65536 | bytes 197632 | tf_op jit(solution)/shard_map/convert_element_type | solution.py:120
  (19 shorter events, 0.2 us)
Async XLA Ops:
  0.7 0.7 copy-start.5
  3.1 14.4 %copy-start.4 = (s32[1,32]{1,0:T(1,128)S(1)}, s32[1,32]{1,0:T(1,128)}, u32[]{:S(2)}) copy-start(s32[1,32]{1,0:T(1,128)} %param.12) | copy-start | bytes 388
  3.1 0.7 copy-start.3
  3.8 13.8 %copy-start.1 = (bf16[1,8,32,128]{3,2,1,0:T(8,128)(2,1)S(1)}, bf16[1,8,32,128]{3,2,1,0:T(8,128)(2,1)}, u32[]{:S(2)}) copy-start(bf16[1,8,32,128]{3,2,1,0:T(8,128)(2,1)} %param.10) | copy-start | bytes 196612
  13.8 17.8 %copy-start = (bf16[1,2,1024,128]{3,2,1,0:T(8,128)(2,1)S(1)}, bf16[1,2,1024,128]{3,2,1,0:T(8,128)(2,1)}, u32[]{:S(2)}) copy-start(bf16[1,2,1024,128]{3,2,1,0:T(8,128)(2,1)} %param.14) | copy-start | bytes 1572868
  34.8 6.4 %copy-start.2 = (bf16[1,2,1024,128]{3,2,1,0:T(8,128)(2,1)S(1)}, bf16[1,2,1024,128]{3,2,1,0:T(8,128)(2,1)}, u32[]{:S(2)}) copy-start(bf16[1,2,1024,128]{3,2,1,0:T(8,128)(2,1)} %param.15) | copy-start | bytes 1572868
  37.1 9.1 %all-to-all-start.2 = ((f32[4,1,256]{2,1,0:T(1,128)}), f32[4,1,256]{2,1,0:T(1,128)S(1)}, u32[]{:S(2)}, u32[]{:S(2)}) async-start(f32[4,1,256]{2,1,0:T(1,128)} %reshape.392), calls=%async_computation.2 | async-start | bytes 8192 | tf_op jit(solution)/shard_map/all_to_all | solution.py:116
  46.2 9.4 %all-to-all-start.1 = ((f32[4,1,256]{2,1,0:T(1,128)}), f32[4,1,256]{2,1,0:T(1,128)S(1)}, u32[]{:S(2)}, u32[]{:S(2)}) async-start(f32[4,1,256]{2,1,0:T(1,128)} %reshape.390), calls=%async_computation.1 | async-start | bytes 8192 | tf_op jit(solution)/shard_map/all_to_all | solution.py:117
  55.5 13.7 %all-to-all-start = ((f32[1,32,2,16,128]{4,3,2,0,1:T(8,128)}), f32[1,32,2,16,128]{4,3,2,0,1:T(8,128)S(1)}, u32[]{:S(2)}, u32[]{:S(2)}) async-start(f32[1,32,2,16,128]{4,3,2,0,1:T(8,128)} %fusion.23), calls=%async_computation | async-start | bytes 1048576 | tf_op jit(solution)/shard_map/all_to_all | solution.py:115
where the time goes:
time: 70.6 us; the launch traced here: 70.2 us
  blocking collectives  23.7 us (34%)
  waiting for transfers between devices  14 us (20%)
  starting transfers between devices  10.8 us (15%)
  local copies, waits for them, and re-layouts  9.41 us (13%)
  other arithmetic  5.07 us (7%)
  matrix products  3.86 us (5%)
  loops' own time  1.9 us (3%)
  between operations  1.49 us (2%)
    all_gather x1, blocking collectives, per_device(): piece_queries = lax.all_gather(queries, 'blk', axis=1, tiled=True)  13.8 us
    unnamed x1, blocking collectives  9.89 us
    all_to_all x1, waiting for transfers between devices, per_device(): lax.all_to_all(merged_out[None], 'blk', split_axis=1, concat_axis=0, tile...  8 us
    all_to_all x1, waiting for transfers between devices, per_device(): lax.all_to_all(merged_top[None], 'blk', split_axis=1, concat_axis=0, tile...  4.68 us
    unnamed x20, local copies, waits for them, and re-layouts  4.28 us
    all_to_all x1, starting transfers between devices, per_device(): lax.all_to_all(merged_top[None], 'blk', split_axis=1, concat_axis=0, tile...  3.79 us
    all_to_all x1, starting transfers between devices, per_device(): lax.all_to_all(merged_tot[None], 'blk', split_axis=1, concat_axis=0, tile...  3.56 us
    all_to_all x1, starting transfers between devices, per_device(): lax.all_to_all(merged_out[None], 'blk', split_axis=1, concat_axis=0, tile...  3.47 us
  transfers between devices with their start and end apart: 3, of which 3 were waited for; matrix products, arithmetic and copies ran while one was open for 10% of the time, Pallas kernels for 0%

commit v1 on v0

v1 whole, which is shorter than its diff:
```python
import functools

import jax
import jax.numpy as jnp
from jax import lax
from jax.experimental import pallas as pl
from jax.experimental.pallas import tpu as pltpu
from jax.sharding import PartitionSpec as P

KB = 256
LANES = 128
MASKED = -1e30
LOW = -32768.0
FINE = 32768.0
STEPS = 32767.0
SCALE_GRID = 1024.0
STATS = 16

VMEM = pl.BlockSpec(memory_space=pltpu.VMEM)
SMEM = pl.BlockSpec(memory_space=pltpu.SMEM)


def partner_pairs(count, step):
    if count & (count - 1) == 0:
        return [(i, i ^ step) for i in range(count)]
    return [(i, (i + step) % count) for i in range(count)]


def send_to(me, count, step):
    return (me ^ step) if count & (count - 1) == 0 else lax.rem(me + step, count)


def got_from(me, count, step):
    return (me ^ step) if count & (count - 1) == 0 else lax.rem(me - step + count, count)


def pack_kernel(positions_ref, lengths_ref, queries_ref, packed_ref, *, tiles):
    rows, heads, width = queries_ref.shape[1:]
    me = lax.axis_index("blk")
    packed_ref[: rows * heads] = queries_ref[0].reshape(rows * heads, width)
    digit = lax.broadcasted_iota(jnp.int32, (16, LANES), 0)
    lane = lax.broadcasted_iota(jnp.int32, (16, LANES), 1)
    own_length = lengths_ref[0]
    for tile in range(tiles):
        place = lane + tile * LANES
        held = jnp.zeros((16, LANES), jnp.int32)
        for row in range(rows):
            held = jnp.where(place == me * rows + row, positions_ref[0, row], held)
        sized = jnp.where(place == me, own_length, 0)
        digits = jnp.where(digit < 3, held, sized)
        third = jnp.where(digit < 3, digit, digit - 3)
        digits = jnp.where(
            third == 0, digits >> 14, jnp.where(third == 1, (digits >> 7) & 127, digits & 127)
        )
        digits = jnp.where(digit < 6, digits, 0)
        packed_ref[pl.ds(rows * heads + tile * 16, 16)] = digits.astype(jnp.float32).astype(jnp.bfloat16)


def attend_kernel(*refs, count, steps, rows, kv_heads, group, tiles, scaling):
    order_ref, lengths_ref, keys_ref, values_ref = refs[:4]
    message_refs = refs[4 : 4 + count]
    out_refs = refs[4 + count : 4 + count + len(steps)]
    held, picked = refs[4 + count + len(steps) :]
    me = lax.axis_index("blk")
    heads = kv_heads * group
    body = rows * heads
    capacity = keys_ref.shape[2]
    for step in range(count):
        held[got_from(me, count, step)] = message_refs[step][...]
    pos, offset = [], jnp.zeros((1, 1), jnp.float32)
    for tile in range(tiles):
        digits = held[0, pl.ds(body + tile * 16, 16)].astype(jnp.float32)
        for other in range(1, count):
            digits += held[other, pl.ds(body + tile * 16, 16)].astype(jnp.float32)
        pos.append(digits[0:1] * 16384.0 + digits[1:2] * 128.0 + digits[2:3])
        sizes = digits[3:4] * 16384.0 + digits[4:5] * 128.0 + digits[5:6]
        lane = lax.broadcasted_iota(jnp.int32, (1, LANES), 1) + tile * LANES
        offset += jnp.sum(jnp.where(lane < me, sizes, 0.0), axis=1, keepdims=True)
    own_length = lengths_ref[0].astype(jnp.float32)
    live = [jnp.clip(p - offset, 0.0, own_length) for p in pos]
    high = [jnp.floor(x * (1.0 / 128.0)) for x in live]
    low = [x - h * 128.0 for x, h in zip(live, high)]
    live_digits = jnp.concatenate(
        [jnp.concatenate([h, l, jnp.zeros((6, LANES), jnp.float32)], axis=0) for h, l in zip(high, low)],
        axis=1,
    ).astype(jnp.bfloat16)
    columns = rows * group
    lane_row = lax.broadcasted_iota(jnp.int32, (1, columns), 1) // group
    spread_row = lax.broadcasted_iota(jnp.int32, (tiles * LANES, columns), 0)
    counts = []
    for at, step in enumerate(steps):
        target = send_to(me, count, step)
        chosen = jnp.zeros((1, columns), jnp.int32)
        for i in range(rows):
            row = order_ref[0, target * rows + i]
            chosen = jnp.where(lane_row == i, row, chosen)
            source = row // rows
            inner = row - source * rows
            for kv in range(kv_heads):
                start = pl.multiple_of(inner * heads + kv * group, group)
                picked[kv, pl.ds(at * columns + i * group, group)] = held[source, pl.ds(start, group)]
        spread = jnp.where(spread_row == chosen, 1.0, 0.0).astype(jnp.bfloat16)
        both = jnp.dot(live_digits, spread, preferred_element_type=jnp.float32)
        counts.append((both[0:1] * 128.0 + both[1:2]).astype(jnp.int32))
    visible_count = jnp.concatenate(counts, axis=1) if len(counts) > 1 else counts[0]

    wide = len(steps) * columns
    slot = lax.broadcasted_iota(jnp.int32, (KB, wide), 0)
    for kv in range(kv_heads):
        query = picked[kv]
        top = jnp.full((1, wide), MASKED, jnp.float32)
        total = jnp.zeros((1, wide), jnp.float32)
        out = jnp.zeros((values_ref.shape[3], wide), jnp.float32)
        for block in range(capacity // KB):
            key_block = keys_ref[0, kv, block * KB : (block + 1) * KB]
            value_block = values_ref[0, kv, block * KB : (block + 1) * KB]
            scores = lax.dot_general(
                key_block, query, (((1,), (1,)), ((), ())), preferred_element_type=jnp.float32
            )
            scores = jnp.where(slot < visible_count - block * KB, scores, MASKED)
            block_top = jnp.max(scores, axis=0, keepdims=True)
            weights = jnp.exp((scores - block_top) * scaling)
            block_total = jnp.sum(weights, axis=0, keepdims=True)
            block_out = lax.dot_general(
                value_block,
                weights.astype(jnp.bfloat16),
                (((0,), (0,)), ((), ())),
                preferred_element_type=jnp.float32,
            )
            joined = jnp.maximum(top, block_top)
            older = jnp.exp((top - joined) * scaling)
            newer = jnp.exp((block_top - joined) * scaling)
            out = out * older + block_out * newer
            total = total * older + block_total * newer
            top = joined
        largest = jnp.max(jnp.abs(out), axis=0, keepdims=True) / total
        grid = jnp.maximum(jnp.ceil(largest * SCALE_GRID), 1.0)
        coded = jnp.round(out * (STEPS * SCALE_GRID / (grid * total)))
        log_sum = jnp.maximum(top * scaling + jnp.log(total), LOW)
        whole = jnp.floor(log_sum)
        part = jnp.floor((log_sum - whole) * FINE)
        stats = jnp.concatenate(
            [whole, part, grid, jnp.zeros((STATS - 3, wide), jnp.float32)], axis=0
        )
        message = jnp.concatenate([coded, stats], axis=0).astype(jnp.int32).astype(jnp.int16)
        for at in range(len(steps)):
            out_refs[at][kv] = message[:, at * columns : (at + 1) * columns]


def settle_kernel(*refs, count, rows, kv_heads, group):
    message_refs, out_ref = refs[:count], refs[count]
    width = out_ref.shape[3]
    for kv in range(kv_heads):
        sums, grids = [], []
        for ref in message_refs:
            stats = ref[kv, width : width + STATS].astype(jnp.float32)
            sums.append(stats[0:1] + stats[1:2] * (1.0 / FINE))
            grids.append(stats[2:3])
        highest = functools.reduce(jnp.maximum, sums)
        shares = [jnp.exp(s - highest) for s in sums]
        whole = functools.reduce(jnp.add, shares)
        result = None
        for ref, share, grid in zip(message_refs, shares, grids):
            term = ref[kv, :width].astype(jnp.float32) * (
                share * grid / (whole * (STEPS * SCALE_GRID))
            )
            result = term if result is None else result + term
        result = result.T.reshape(rows, group, width).astype(jnp.bfloat16)
        out_ref[0, :, kv * group : (kv + 1) * group] = result


def per_device(queries, positions, row_order, lengths, cache_keys, cache_values):
    count = lax.axis_size("blk")
    kv_heads, head_dim = cache_keys.shape[1], cache_keys.shape[3]
    rows, heads = queries.shape[1], queries.shape[2]
    group = heads // kv_heads
    tiles = pl.cdiv(count * rows, LANES)
    packed_rows = rows * heads + 16 * tiles
    columns = rows * group
    packed = pl.pallas_call(
        functools.partial(pack_kernel, tiles=tiles),
        out_shape=jax.ShapeDtypeStruct((packed_rows, head_dim), jnp.bfloat16),
        in_specs=[SMEM, SMEM, VMEM],
        out_specs=VMEM,
    )(positions, lengths, queries)
    messages = [packed] + [
        lax.ppermute(packed, "blk", partner_pairs(count, step)) for step in range(1, count)
    ]
    steps = list(range(count))
    parts = pl.pallas_call(
        functools.partial(
            attend_kernel,
            count=count,
            steps=steps,
            rows=rows,
            kv_heads=kv_heads,
            group=group,
            tiles=tiles,
            scaling=float(head_dim) ** -0.5,
        ),
        out_shape=[
            jax.ShapeDtypeStruct((kv_heads, head_dim + STATS, columns), jnp.int16) for _ in steps
        ],
        in_specs=[SMEM, SMEM, VMEM, VMEM] + [VMEM] * count,
        out_specs=[VMEM] * len(steps),
        scratch_shapes=[
            pltpu.VMEM((count, packed_rows, head_dim), jnp.bfloat16),
            pltpu.VMEM((kv_heads, len(steps) * columns, head_dim), jnp.bfloat16),
        ],
        compiler_params=pltpu.CompilerParams(vmem_limit_bytes=32 << 20),
    )(row_order, lengths, cache_keys, cache_values, *messages)
    gathered = [parts[0]] + [
        lax.ppermute(parts[step], "blk", partner_pairs(count, step)) for step in range(1, count)
    ]
    return pl.pallas_call(
        functools.partial(settle_kernel, count=count, rows=rows, kv_heads=kv_heads, group=group),
        out_shape=jax.ShapeDtypeStruct((1, rows, heads, head_dim), jnp.bfloat16),
        in_specs=[VMEM] * count,
        out_specs=VMEM,
    )(*gathered)


def solution(mesh):
    placed = (
        P(("groups", "beam"), "blk", "heads", None),
        P(("groups", "beam"), "blk"),
        P(("groups", "beam"), None),
        P(("groups", "blk")),
        P(("groups", "blk"), "heads", None, None),
        P(("groups", "blk"), "heads", None, None),
    )
    return jax.shard_map(
        per_device,
        mesh=mesh,
        in_specs=placed,
        out_specs=P(("groups", "beam"), "blk", "heads", None),
        check_vma=False,
    )
```

time: 70.6 us -> 33.2 us (0.47)
  blocking collectives: 23.7 us -> 0 us
  Pallas kernels: 0 us -> 7.28 us
  local copies, waits for them, and re-layouts: 9.41 us -> 4.21 us
  other arithmetic: 5.07 us -> 0 us
  matrix products: 3.86 us -> 0 us
  waiting for transfers between devices: 14 us -> 10.6 us
  loops' own time: 1.9 us -> 0 us
  starting transfers between devices: 10.8 us -> 10 us
  between operations: 1.49 us -> 0.69 us
    all_to_all x3 -> x0, waiting for transfers between devices: 14 us -> none  [the longest x1 8 us: per_device(): lax.all_to_all(merged_out[None], 'blk', split_axis=1, concat_axis=0, tile...]
    all_gather x1 -> x0, blocking collectives: 13.8 us -> none  [per_device(): piece_queries = lax.all_gather(queries, 'blk', axis=1, tiled=True)]
    all_to_all x3 -> x0, starting transfers between devices: 10.8 us -> none  [the longest x1 3.79 us: per_device(): lax.all_to_all(merged_top[None], 'blk', split_axis=1, concat_axis=0, tile...]
    ppermute x0 -> x6, waiting for transfers between devices: none -> 10.6 us  [the longest x3 5.55 us: per_device(): lax.ppermute(packed, 'blk', partner_pairs(count, step))]
    ppermute x0 -> x6, starting transfers between devices: none -> 10 us  [the longest x3 5.62 us: per_device(): lax.ppermute(packed, 'blk', partner_pairs(count, step))]
    unnamed x1 -> x0, blocking collectives: 9.89 us -> none
    pallas_call x0 -> x3, Pallas kernels: none -> 7.28 us  [the longest x1 4.01 us: per_device(): pl.pallas_call(functools.partial(attend_kernel, count=count, steps=steps,...]
    dot_general x8 -> x0, matrix products: 3.86 us -> none  [the longest x4 2.34 us: block_partial(): jnp.einsum('rkgj,kjd->rkgd', weights.astype(jnp.bfloat16), value_block, p...]
  transfers between devices with their start and end apart: 3 -> 6, of which waited for: 3 -> 5; matrix products, arithmetic and copies ran while one was open for 10% -> 0% of each run, Pallas kernels for 0% -> 0%
where the time goes in v1:
time: 33.2 us; the launch traced here: 32.8 us
  waiting for transfers between devices  10.6 us (32%)
  starting transfers between devices  10 us (30%)
  Pallas kernels  7.28 us (22%)
  local copies, waits for them, and re-layouts  4.21 us (13%)
  between operations  0.69 us (2%)
    ppermute x3, starting transfers between devices, per_device(): lax.ppermute(packed, 'blk', partner_pairs(count, step))  5.62 us
    ppermute x3, waiting for transfers between devices, per_device(): lax.ppermute(packed, 'blk', partner_pairs(count, step))  5.55 us
    ppermute x3, waiting for transfers between devices, per_device(): lax.ppermute(parts[step], 'blk', partner_pairs(count, step))  5.07 us
    ppermute x3, starting transfers between devices, per_device(): lax.ppermute(parts[step], 'blk', partner_pairs(count, step))  4.39 us
    unnamed x16, local copies, waits for them, and re-layouts  4.21 us
    pallas_call x1, Pallas kernels, per_device(): pl.pallas_call(functools.partial(attend_kernel, count=count, steps=steps,...  4.01 us
    pallas_call x1, Pallas kernels, per_device(): pl.pallas_call(functools.partial(settle_kernel, count=count, rows=rows, k...  1.78 us
    pallas_call x1, Pallas kernels, per_device(): pl.pallas_call(functools.partial(pack_kernel, tiles=tiles), out_shape=jax...  1.49 us
  transfers between devices with their start and end apart: 6, of which 5 were waited for; matrix products, arithmetic and copies ran while one was open for 0% of the time, Pallas kernels for 0%

profile of v1, /device:TPU:0, one launch (start us, length us, event | category | flops | bytes accessed | tf_op | source)
XLA Modules:
  0.0 32.8 jit_solution(12032624845299547846)
XLA Ops:
  0.7 0.0 copy-start.4
  0.7 1.5 %shard_map.64.refs_4_ = bf16[272,128]{1,0:T(8,128)(2,1)} custom-call(s32[1,8]{1,0:T(1,128)} %positions_ref.1, s32[1]{0:T(128)S(6)} %copy.7.lengths_ref.refs_1_, bf16[1,8,32,128]{3,2,1,0:T(8,128)(2,1)} %queries_ref.1), custom_call_target="tpu_custom_call" | custom-call | tf_op jit(solution)/shard_map/pallas_call | solution.py:180
  2.2 5.0 %collective-permute-start.2 = (bf16[272,128]{1,0:T(8,128)(2,1)}, bf16[272,128]{1,0:T(8,128)(2,1)S(1)}, u32[]{:S(2)}, u32[]{:S(2)}) collective-permute-start(bf16[272,128]{1,0:T(8,128)(2,1)} %shard_map.64.refs_4_), channel_id=1, source_target_pairs={{0,12},{4,8},{8,4},{12,0},{1,13},{5,9},{9,5},{13,1},{2,14},{6,10},... | collective-permute-start | bytes 208904 | tf_op jit(solution)/shard_map/ppermute | solution.py:187
  7.2 0.0 collective-permute-start.1
  7.2 0.6 %collective-permute-start = (bf16[272,128]{1,0:T(8,128)(2,1)}, bf16[272,128]{1,0:T(8,128)(2,1)S(1)}, u32[]{:S(2)}, u32[]{:S(2)}) collective-permute-start(bf16[272,128]{1,0:T(8,128)(2,1)} %shard_map.64.refs_4_), channel_id=1, source_target_pairs={{0,4},{4,0},{8,12},{12,8},{1,5},{5,1},{9,13},{13,9},{2,6},{6,2},{1... | collective-permute-start | bytes 208904 | tf_op jit(solution)/shard_map/ppermute | solution.py:187
  7.8 2.3 %collective-permute-done.2.refs_7_ = bf16[272,128]{1,0:T(8,128)(2,1)S(1)} collective-permute-done((bf16[272,128]{1,0:T(8,128)(2,1)}, bf16[272,128]{1,0:T(8,128)(2,1)S(1)}, u32[]{:S(2)}, u32[]{:S(2)}) %collective-permute-start.2) | collective-permute-done | bytes 69664 | tf_op jit(solution)/shard_map/ppermute | solution.py:187
  10.1 3.2 %collective-permute-done.1.refs_6_ = bf16[272,128]{1,0:T(8,128)(2,1)S(1)} collective-permute-done((bf16[272,128]{1,0:T(8,128)(2,1)}, bf16[272,128]{1,0:T(8,128)(2,1)S(1)}, u32[]{:S(2)}, u32[]{:S(2)}) %collective-permute-start.1) | collective-permute-done | bytes 69664 | tf_op jit(solution)/shard_map/ppermute | solution.py:187
  13.3 0.0 collective-permute-done.refs_5_
  13.3 0.0 copy-done.4
  13.3 0.0 copy-start
  13.3 1.0 %copy-done = bf16[1,2,1024,128]{3,2,1,0:T(8,128)(2,1)S(1)} copy-done((bf16[1,2,1024,128]{3,2,1,0:T(8,128)(2,1)S(1)}, bf16[1,2,1024,128]{3,2,1,0:T(8,128)(2,1)}, u32[]{:S(2)}) %copy-start) | copy-done | bytes 524312
  14.4 0.0 copy-start.1
  14.4 1.0 %copy-done.1 = bf16[1,2,1024,128]{3,2,1,0:T(8,128)(2,1)S(1)} copy-done((bf16[1,2,1024,128]{3,2,1,0:T(8,128)(2,1)S(1)}, bf16[1,2,1024,128]{3,2,1,0:T(8,128)(2,1)}, u32[]{:S(2)}) %copy-start.1) | copy-done | bytes 524312
  15.4 0.0 copy-start.2
  15.4 0.9 %copy-done.2 = bf16[272,128]{1,0:T(8,128)(2,1)S(1)} copy-done((bf16[272,128]{1,0:T(8,128)(2,1)S(1)}, bf16[272,128]{1,0:T(8,128)(2,1)}, u32[]{:S(2)}) %copy-start.2) | copy-done | bytes 69656
  16.3 4.0 %shard_map.65 = (s16[2,144,128]{2,1,0:T(8,128)(2,1)S(1)}, s16[2,144,128]{2,1,0:T(8,128)(2,1)S(1)}, s16[2,144,128]{2,1,0:T(8,128)(2,1)S(1)}, s16[2,144,128]{2,1,0:T(8,128)(2,1)S(1)}) custom-call(s32[1,32]{1,0:T(1,128)S(1)} %copy-done.4, s32[1]{0:T(128)S(6)} %copy.7.lengths_ref.refs_1_, bf16[1,2,1024,128]{3,2,1,0:T(8,128)(2,1)S(1)} %copy-done, ...), custom_call_target="tpu_custom_call" | custom-call | tf_op jit(solution)/shard_map/pallas_call | solution.py:190
  20.3 0.0 copy-start.3
  20.3 0.6 %copy-done.3 = s16[2,144,128]{2,1,0:T(8,128)(2,1)} copy-done((s16[2,144,128]{2,1,0:T(8,128)(2,1)}, s16[2,144,128]{2,1,0:T(8,128)(2,1)S(1)}, u32[]{:S(2)}) %copy-start.3) | copy-done | bytes 73752
  20.9 1.0 %collective-permute-start.3 = (s16[2,144,128]{2,1,0:T(8,128)(2,1)S(1)}, s16[2,144,128]{2,1,0:T(8,128)(2,1)S(1)}, u32[]{:S(2)}, u32[]{:S(2)}) collective-permute-start(s16[2,144,128]{2,1,0:T(8,128)(2,1)S(1)} %get-tuple-element.10), channel_id=1, source_target_pairs={{0,4},{4,0},{8,12},{12,8},{1,5},{5,1},{9,13},{13,9},{2,6},{6,2},{1... | collective-permute-start | bytes 221192 | tf_op jit(solution)/shard_map/ppermute | solution.py:213
  22.0 2.2 %collective-permute-start.4 = (s16[2,144,128]{2,1,0:T(8,128)(2,1)S(1)}, s16[2,144,128]{2,1,0:T(8,128)(2,1)S(1)}, u32[]{:S(2)}, u32[]{:S(2)}) collective-permute-start(s16[2,144,128]{2,1,0:T(8,128)(2,1)S(1)} %get-tuple-element.11), channel_id=1, source_target_pairs={{0,8},{4,12},{8,0},{12,4},{1,9},{5,13},{9,1},{13,5},{2,10},{6,14},... | collective-permute-start | bytes 221192 | tf_op jit(solution)/shard_map/ppermute | solution.py:213
  24.1 1.2 %collective-permute-start.5 = (s16[2,144,128]{2,1,0:T(8,128)(2,1)S(1)}, s16[2,144,128]{2,1,0:T(8,128)(2,1)S(1)}, u32[]{:S(2)}, u32[]{:S(2)}) collective-permute-start(s16[2,144,128]{2,1,0:T(8,128)(2,1)S(1)} %get-tuple-element.12), channel_id=1, source_target_pairs={{0,12},{4,8},{8,4},{12,0},{1,13},{5,9},{9,5},{13,1},{2,14},{6,10},... | collective-permute-start | bytes 221192 | tf_op jit(solution)/shard_map/ppermute | solution.py:213
  25.3 0.2 collective-permute-done.3.refs_1_
  25.5 0.0 copy-start.5
  25.5 3.3 %collective-permute-done.4.refs_2_ = s16[2,144,128]{2,1,0:T(8,128)(2,1)S(1)} collective-permute-done((s16[2,144,128]{2,1,0:T(8,128)(2,1)S(1)}, s16[2,144,128]{2,1,0:T(8,128)(2,1)S(1)}, u32[]{:S(2)}, u32[]{:S(2)}) %collective-permute-start.4) | collective-permute-done | bytes 73760 | tf_op jit(solution)/shard_map/ppermute | solution.py:213
  28.9 0.0 copy-start.6
  28.9 1.5 %collective-permute-done.5.refs_3_ = s16[2,144,128]{2,1,0:T(8,128)(2,1)S(1)} collective-permute-done((s16[2,144,128]{2,1,0:T(8,128)(2,1)S(1)}, s16[2,144,128]{2,1,0:T(8,128)(2,1)S(1)}, u32[]{:S(2)}, u32[]{:S(2)}) %collective-permute-start.5) | collective-permute-done | bytes 73760 | tf_op jit(solution)/shard_map/ppermute | solution.py:213
  30.4 0.0 copy-start.7
  30.4 0.0 copy-done.5
  30.4 0.0 copy-done.6
  30.4 0.6 %copy-done.7 = s16[2,144,128]{2,1,0:T(8,128)(2,1)} copy-done((s16[2,144,128]{2,1,0:T(8,128)(2,1)}, s16[2,144,128]{2,1,0:T(8,128)(2,1)S(1)}, u32[]{:S(2)}) %copy-start.7) | copy-done | bytes 73752
  31.0 1.8 %shard_map.66 = bf16[1,8,32,128]{3,2,1,0:T(8,128)(2,1)} custom-call(s16[2,144,128]{2,1,0:T(8,128)(2,1)} %copy-done.3, s16[2,144,128]{2,1,0:T(8,128)(2,1)} %copy-done.5, s16[2,144,128]{2,1,0:T(8,128)(2,1)} %copy-done.6, s16[2,144,128]{2,1,0:T(8,128)(2,1)} %copy-done.7), custom_call_target="tpu_custom_call" | custom-call | tf_op jit(solution)/shard_map/pallas_call | solution.py:215
Async XLA Ops:
  0.7 12.7 %copy-start.4 = (s32[1,32]{1,0:T(1,128)S(1)}, s32[1,32]{1,0:T(1,128)}, u32[]{:S(2)}) copy-start(s32[1,32]{1,0:T(1,128)} %refs_0_.1) | copy-start | bytes 388
  2.2 8.0 %collective-permute-start.2 = (bf16[272,128]{1,0:T(8,128)(2,1)}, bf16[272,128]{1,0:T(8,128)(2,1)S(1)}, u32[]{:S(2)}, u32[]{:S(2)}) collective-permute-start(bf16[272,128]{1,0:T(8,128)(2,1)} %shard_map.64.refs_4_), channel_id=1, source_target_pairs={{0,12},{4,8},{8,4},{12,0},{1,13},{5,9},{9,5},{13,1},{2,14},{6,10},... | collective-permute-start | bytes 208904 | tf_op jit(solution)/shard_map/ppermute | solution.py:187
  7.2 6.1 %collective-permute-start.1 = (bf16[272,128]{1,0:T(8,128)(2,1)}, bf16[272,128]{1,0:T(8,128)(2,1)S(1)}, u32[]{:S(2)}, u32[]{:S(2)}) collective-permute-start(bf16[272,128]{1,0:T(8,128)(2,1)} %shard_map.64.refs_4_), channel_id=1, source_target_pairs={{0,8},{4,12},{8,0},{12,4},{1,9},{5,13},{9,1},{13,5},{2,10},{6,14},... | collective-permute-start | bytes 208904 | tf_op jit(solution)/shard_map/ppermute | solution.py:187
  7.2 6.1 %collective-permute-start = (bf16[272,128]{1,0:T(8,128)(2,1)}, bf16[272,128]{1,0:T(8,128)(2,1)S(1)}, u32[]{:S(2)}, u32[]{:S(2)}) collective-permute-start(bf16[272,128]{1,0:T(8,128)(2,1)} %shard_map.64.refs_4_), channel_id=1, source_target_pairs={{0,4},{4,0},{8,12},{12,8},{1,5},{5,1},{9,13},{13,9},{2,6},{6,2},{1... | collective-permute-start | bytes 208904 | tf_op jit(solution)/shard_map/ppermute | solution.py:187
  13.3 1.0 %copy-start = (bf16[1,2,1024,128]{3,2,1,0:T(8,128)(2,1)S(1)}, bf16[1,2,1024,128]{3,2,1,0:T(8,128)(2,1)}, u32[]{:S(2)}) copy-start(bf16[1,2,1024,128]{3,2,1,0:T(8,128)(2,1)} %refs_2_.1) | copy-start | bytes 1572868
  14.4 1.0 %copy-start.1 = (bf16[1,2,1024,128]{3,2,1,0:T(8,128)(2,1)S(1)}, bf16[1,2,1024,128]{3,2,1,0:T(8,128)(2,1)}, u32[]{:S(2)}) copy-start(bf16[1,2,1024,128]{3,2,1,0:T(8,128)(2,1)} %refs_3_.1) | copy-start | bytes 1572868
  15.4 0.9 %copy-start.2 = (bf16[272,128]{1,0:T(8,128)(2,1)S(1)}, bf16[272,128]{1,0:T(8,128)(2,1)}, u32[]{:S(2)}) copy-start(bf16[272,128]{1,0:T(8,128)(2,1)} %shard_map.64.refs_4_) | copy-start | bytes 208900
  20.3 0.6 %copy-start.3 = (s16[2,144,128]{2,1,0:T(8,128)(2,1)}, s16[2,144,128]{2,1,0:T(8,128)(2,1)S(1)}, u32[]{:S(2)}) copy-start(s16[2,144,128]{2,1,0:T(8,128)(2,1)S(1)} %get-tuple-element.9.refs_0_) | copy-start | bytes 221188
  20.9 4.6 %collective-permute-start.3 = (s16[2,144,128]{2,1,0:T(8,128)(2,1)S(1)}, s16[2,144,128]{2,1,0:T(8,128)(2,1)S(1)}, u32[]{:S(2)}, u32[]{:S(2)}) collective-permute-start(s16[2,144,128]{2,1,0:T(8,128)(2,1)S(1)} %get-tuple-element.10), channel_id=1, source_target_pairs={{0,4},{4,0},{8,12},{12,8},{1,5},{5,1},{9,13},{13,9},{2,6},{6,2},{1... | collective-permute-start | bytes 221192 | tf_op jit(solution)/shard_map/ppermute | solution.py:213
  22.0 6.9 %collective-permute-start.4 = (s16[2,144,128]{2,1,0:T(8,128)(2,1)S(1)}, s16[2,144,128]{2,1,0:T(8,128)(2,1)S(1)}, u32[]{:S(2)}, u32[]{:S(2)}) collective-permute-start(s16[2,144,128]{2,1,0:T(8,128)(2,1)S(1)} %get-tuple-element.11), channel_id=1, source_target_pairs={{0,8},{4,12},{8,0},{12,4},{1,9},{5,13},{9,1},{13,5},{2,10},{6,14},... | collective-permute-start | bytes 221192 | tf_op jit(solution)/shard_map/ppermute | solution.py:213
  24.1 6.3 %collective-permute-start.5 = (s16[2,144,128]{2,1,0:T(8,128)(2,1)S(1)}, s16[2,144,128]{2,1,0:T(8,128)(2,1)S(1)}, u32[]{:S(2)}, u32[]{:S(2)}) collective-permute-start(s16[2,144,128]{2,1,0:T(8,128)(2,1)S(1)} %get-tuple-element.12), channel_id=1, source_target_pairs={{0,12},{4,8},{8,4},{12,0},{1,13},{5,9},{9,5},{13,1},{2,14},{6,10},... | collective-permute-start | bytes 221192 | tf_op jit(solution)/shard_map/ppermute | solution.py:213
  25.5 4.9 %copy-start.5 = (s16[2,144,128]{2,1,0:T(8,128)(2,1)}, s16[2,144,128]{2,1,0:T(8,128)(2,1)S(1)}, u32[]{:S(2)}) copy-start(s16[2,144,128]{2,1,0:T(8,128)(2,1)S(1)} %collective-permute-done.3.refs_1_) | copy-start | bytes 221188
  28.9 1.5 %copy-start.6 = (s16[2,144,128]{2,1,0:T(8,128)(2,1)}, s16[2,144,128]{2,1,0:T(8,128)(2,1)S(1)}, u32[]{:S(2)}) copy-start(s16[2,144,128]{2,1,0:T(8,128)(2,1)S(1)} %collective-permute-done.4.refs_2_) | copy-start | bytes 221188
  30.4 0.6 %copy-start.7 = (s16[2,144,128]{2,1,0:T(8,128)(2,1)}, s16[2,144,128]{2,1,0:T(8,128)(2,1)S(1)}, u32[]{:S(2)}) copy-start(s16[2,144,128]{2,1,0:T(8,128)(2,1)S(1)} %collective-permute-done.5.refs_3_) | copy-start | bytes 221188

commit v2 on v1

v2 whole, which is shorter than its diff:
```python
import functools
import math

import jax
import jax.numpy as jnp
from jax import lax
from jax.experimental import pallas as pl
from jax.experimental.pallas import tpu as pltpu
from jax.sharding import PartitionSpec as P

KB = 256
LANES = 128
MASKED = -1e30
LOW = -32768.0
FINE = 32768.0
STEPS = 32767.0
SCALE_GRID = 1024.0
STATS = 16

VMEM = pl.BlockSpec(memory_space=pltpu.VMEM)
SMEM = pl.BlockSpec(memory_space=pltpu.SMEM)
HBM = pl.BlockSpec(memory_space=pltpu.HBM)


def shift_pairs(count, step):
    return [(i, (i + step) % count) for i in range(count)]


def first_source(me, count, step):
    return lax.rem(me - step + count, count)


def second_target(me, count, step):
    return lax.rem(me + step, count)


def in_hbm(*arrays):
    return [pltpu.with_memory_space_constraint(array, pltpu.HBM) for array in arrays]


def pack_kernel(
    lengths_ref, positions_ref, queries_ref, packed_ref, positions, sems, *, tiles
):
    rows, heads, width = queries_ref.shape[1:]
    me = lax.axis_index("blk")
    copies = [
        pltpu.make_async_copy(positions_ref, positions, sems.at[0]),
    ] + [
        pltpu.make_async_copy(
            queries_ref.at[0, row], packed_ref.at[pl.ds(row * heads, heads)], sems.at[1 + row]
        )
        for row in range(rows)
    ]
    for copy in copies:
        copy.start()
    digit = lax.broadcasted_iota(jnp.int32, (16, LANES), 0)
    lane = lax.broadcasted_iota(jnp.int32, (16, LANES), 1)
    copies[0].wait()
    own_length = lengths_ref[0]
    for tile in range(tiles):
        place = lane + tile * LANES
        held = jnp.zeros((16, LANES), jnp.int32)
        for row in range(rows):
            held = jnp.where(place == me * rows + row, positions[0, row], held)
        sized = jnp.where(place == me, own_length, 0)
        digits = jnp.where(digit < 3, held, sized)
        third = jnp.where(digit < 3, digit, digit - 3)
        digits = jnp.where(
            third == 0, digits >> 14, jnp.where(third == 1, (digits >> 7) & 127, digits & 127)
        )
        digits = jnp.where(digit < 6, digits, 0)
        packed_ref[pl.ds(rows * heads + tile * 16, 16)] = digits.astype(jnp.float32).astype(jnp.bfloat16)
    for copy in copies[1:]:
        copy.wait()


def stage_kernel(*refs, count, plan, rows, group):
    keys_ref, values_ref, order_ref = refs[:3]
    keys_out_ref, values_out_ref, order_out_ref, spread_ref = refs[3:7]
    held, order, sems = refs[7:]
    kv_heads, pieces, part = held.shape[:3]
    me = lax.axis_index("blk")
    order_copies = [
        pltpu.make_async_copy(order_ref, order, sems.at[2, 0, 0]),
        pltpu.make_async_copy(order_ref, order_out_ref, sems.at[2, 0, 1]),
    ]
    for copy in order_copies:
        copy.start()
    copies = {}
    for kv in range(kv_heads):
        for piece in range(pieces):
            at = pl.ds(piece * part, part)
            copies[1, kv, piece] = pltpu.make_async_copy(
                values_ref.at[0, kv, at], held.at[kv, piece], sems.at[1, kv, piece]
            )
            copies[0, kv, piece] = pltpu.make_async_copy(
                keys_ref.at[0, kv, at], keys_out_ref.at[kv, at], sems.at[0, kv, piece]
            )
            copies[1, kv, piece].start()
            copies[0, kv, piece].start()
    for copy in order_copies:
        copy.wait()
    columns = rows * group
    lane_row = lax.broadcasted_iota(jnp.int32, (1, columns), 1) // group
    spread_row = lax.broadcasted_iota(jnp.int32, (spread_ref.shape[0], columns), 0)
    for at, step in enumerate(sum(plan, [])):
        chosen = jnp.zeros((1, columns), jnp.int32)
        for i in range(rows):
            chosen = jnp.where(lane_row == i, order[0, second_target(me, count, step) * rows + i], chosen)
        spread = jnp.where(spread_row == chosen, 1.0, 0.0).astype(jnp.bfloat16)
        spread_ref[:, at * columns : (at + 1) * columns] = spread
    for kv in range(kv_heads):
        for piece in range(pieces):
            copies[1, kv, piece].wait()
            values_out_ref[kv, :, piece * part : (piece + 1) * part] = held[kv, piece].T
            copies[0, kv, piece].wait()


def attend(keys_ref, values_ref, asked, counts, out_refs, scores, scaling):
    kv_heads, capacity, wide = scores.shape
    columns = wide // len(out_refs)
    head_dim = values_ref.shape[1]
    slot = lax.broadcasted_iota(jnp.int32, (KB, wide), 0)
    rate = scaling * math.log2(math.e)
    for kv in range(kv_heads):
        scores[kv] = lax.dot_general(
            keys_ref[kv], asked[kv], (((1,), (1,)), ((), ())), preferred_element_type=jnp.float32
        )
    stats = []
    for kv in range(kv_heads):
        tops, totals, outs = [], [], []
        for block in range(capacity // KB):
            at = pl.ds(block * KB, KB)
            seen = jnp.where(slot < counts - block * KB, scores[kv, at], MASKED)
            top = jnp.max(seen, axis=0, keepdims=True)
            weights = jnp.exp2((seen - top) * rate)
            tops.append(top)
            totals.append(jnp.sum(weights, axis=0, keepdims=True))
            outs.append(
                jnp.dot(
                    values_ref[kv, :, at], weights.astype(jnp.bfloat16), preferred_element_type=jnp.float32
                )
            )
        top = functools.reduce(jnp.maximum, tops)
        factors = [jnp.exp2((t - top) * rate) for t in tops]
        total = functools.reduce(jnp.add, [f * t for f, t in zip(factors, totals)])
        out = functools.reduce(jnp.add, [f * o for f, o in zip(factors, outs)])
        largest = jnp.max(jnp.abs(out), axis=0, keepdims=True) / total
        grid = jnp.maximum(jnp.ceil(largest * SCALE_GRID), 1.0)
        coded = jnp.round(out * (STEPS * SCALE_GRID / (grid * total)))
        log_sum = jnp.maximum(top * scaling + jnp.log(total), LOW)
        whole = jnp.floor(log_sum)
        part = jnp.floor((log_sum - whole) * FINE)
        stats += [whole, part, grid]
        coded = coded.astype(jnp.int32).astype(jnp.int16)
        for at, ref in enumerate(out_refs):
            ref[kv * head_dim : (kv + 1) * head_dim] = coded[:, at * columns : (at + 1) * columns]
    spare = out_refs[0].shape[0] - kv_heads * head_dim - len(stats)
    stats = jnp.concatenate(stats + [jnp.zeros((spare, wide), jnp.float32)], axis=0)
    stats = stats.astype(jnp.int32).astype(jnp.int16)
    for at, ref in enumerate(out_refs):
        ref[kv_heads * head_dim :] = stats[:, at * columns : (at + 1) * columns]


def first_kernel(*refs, count, plan, rows, group, scaling):
    order_ref, keys_ref, values_ref, spread_ref = refs[:4]
    message_refs = refs[4 : 4 + count]
    asked_ref, counts_ref = refs[4 + count : 6 + count]
    out_refs, held, scores = refs[6 + count : -2], refs[-2], refs[-1]
    me = lax.axis_index("blk")
    kv_heads, _, wide = scores.shape
    columns = rows * group
    heads = kv_heads * group
    body = held.shape[1]
    tiles = spread_ref.shape[0] // LANES
    for step, ref in zip(first_order(count), message_refs):
        held[first_source(me, count, step)] = ref[:body]
    offset = jnp.zeros((1, 1), jnp.float32)
    own_length = jnp.zeros((1, 1), jnp.float32)
    pos = []
    for tile in range(tiles):
        at = pl.ds(body + tile * 16, 16)
        digits = functools.reduce(jnp.add, [ref[at].astype(jnp.float32) for ref in message_refs])
        pos.append(digits[0:1] * 16384.0 + digits[1:2] * 128.0 + digits[2:3])
        sizes = digits[3:4] * 16384.0 + digits[4:5] * 128.0 + digits[5:6]
        lane = lax.broadcasted_iota(jnp.int32, (1, LANES), 1) + tile * LANES
        offset += jnp.sum(jnp.where(lane < me, sizes, 0.0), axis=1, keepdims=True)
        own_length += jnp.sum(jnp.where(lane == me, sizes, 0.0), axis=1, keepdims=True)
    live = jnp.minimum(jnp.maximum(jnp.concatenate(pos, axis=1) - offset, 0.0), own_length)
    high = jnp.floor(live * (1.0 / 128.0))
    live_digits = jnp.concatenate(
        [high, live - high * 128.0, jnp.zeros((14, tiles * LANES), jnp.float32)], axis=0
    ).astype(jnp.bfloat16)
    both = jnp.dot(live_digits, spread_ref[...], preferred_element_type=jnp.float32)
    counts = (both[0:1] * 128.0 + both[1:2]).astype(jnp.int32)
    counts_ref[...] = jnp.broadcast_to(counts, counts_ref.shape)
    asked = [[] for _ in range(kv_heads)]
    for at, step in enumerate(sum(plan, [])):
        for i in range(rows):
            row = order_ref[0, second_target(me, count, step) * rows + i]
            source = lax.div(row, rows)
            inner = row - source * rows
            for kv in range(kv_heads):
                start = pl.multiple_of(inner * heads + kv * group, group)
                query = held[source, pl.ds(start, group)]
                asked_ref[kv, pl.ds(at * columns + i * group, group)] = query
                if at < len(out_refs):
                    asked[kv].append(query)
    asked = [jnp.concatenate(queries, axis=0) for queries in asked]
    attend(keys_ref, values_ref, asked, counts[:, :wide], out_refs, scores, scaling)


def next_kernel(*refs, start, scaling):
    keys_ref, values_ref, asked_ref, counts_ref = refs[:4]
    out_refs, scores = refs[4:-1], refs[-1]
    kv_heads, _, wide = scores.shape
    asked = [asked_ref[kv, pl.ds(start, wide)] for kv in range(kv_heads)]
    counts = counts_ref[0:1, start : start + wide]
    attend(keys_ref, values_ref, asked, counts, out_refs, scores, scaling)


def settle_kernel(*refs, messages, first, last, kv_heads, width, group):
    message_refs, refs = refs[:messages], refs[messages:]
    if not first:
        out_ref, stat_ref, refs = refs[0], refs[1], refs[2:]
    columns = message_refs[0].shape[1]
    all_stats = [ref[kv_heads * width :].astype(jnp.float32) for ref in message_refs]
    for kv in range(kv_heads):
        sums = [s[3 * kv : 3 * kv + 1] + s[3 * kv + 1 : 3 * kv + 2] * (1.0 / FINE) for s in all_stats]
        grids = [s[3 * kv + 2 : 3 * kv + 3] for s in all_stats]
        tops = sums if first else sums + [stat_ref[kv, 0:1]]
        highest = functools.reduce(jnp.maximum, tops)
        shares = [jnp.exp(s - highest) for s in tops]
        total, result = None, None
        if not first:
            total = shares[-1] * stat_ref[kv, 1:2]
            result = shares[-1] * out_ref[kv]
        for ref, share, grid in zip(message_refs, shares, grids):
            held = ref[kv * width : (kv + 1) * width].astype(jnp.float32)
            term = held * (share * grid * (1.0 / (STEPS * SCALE_GRID)))
            total = share if total is None else total + share
            result = term if result is None else result + term
        if last:
            result = (result / total).T.reshape(columns // group, group, width)
            refs[0][0, :, kv * group : (kv + 1) * group] = result.astype(jnp.bfloat16)
        else:
            refs[0][kv] = result
            refs[1][kv] = jnp.concatenate([highest, total, jnp.zeros((6, columns), jnp.float32)], axis=0)


def first_order(count):
    return [0] + list(reversed(range(1, count)))


STAGE_COST = 16777216
OWN_COST = 1
ATTEND_COST = 1
JOIN_COST = 1


def exchange_plan(count):
    later = sorted(range(1, count), key=lambda step: (abs(2 * step - count), step)) + [0]
    chunk = pl.cdiv(count, 4)
    return [later[i : i + chunk] for i in range(0, count, chunk)]


def join_plan(plan):
    return [plan[-1] + plan[0]] + plan[1:-1]


def cost_of(flops):
    return pl.CostEstimate(flops=int(flops), bytes_accessed=1, transcendentals=0)


def per_device(queries, positions, row_order, lengths, cache_keys, cache_values):
    count = lax.axis_size("blk")
    kv_heads, capacity, head_dim = cache_keys.shape[1:]
    rows, heads = queries.shape[1], queries.shape[2]
    group = heads // kv_heads
    tiles = pl.cdiv(count * rows, LANES)
    body = rows * heads
    columns = rows * group
    scaling = float(head_dim) ** -0.5
    packed = pl.pallas_call(
        functools.partial(pack_kernel, tiles=tiles),
        out_shape=jax.ShapeDtypeStruct((body + 16 * tiles, head_dim), jnp.bfloat16),
        in_specs=[SMEM, HBM, HBM],
        out_specs=VMEM,
        scratch_shapes=[
            pltpu.SMEM(positions.shape, jnp.int32),
            pltpu.SemaphoreType.DMA((1 + rows,)),
        ],
        compiler_params=pltpu.CompilerParams(vmem_limit_bytes=4 << 20),
    )(lengths, *in_hbm(positions, queries))
    arrived = {
        step: lax.ppermute(packed, "blk", shift_pairs(count, step)) for step in range(1, count)
    }

    plan = exchange_plan(count)
    pieces = capacity // KB
    staged_keys, staged_values, order, spread = pl.pallas_call(
        functools.partial(stage_kernel, count=count, plan=plan, rows=rows, group=group),
        out_shape=[
            jax.ShapeDtypeStruct((kv_heads, capacity, head_dim), jnp.bfloat16),
            jax.ShapeDtypeStruct((kv_heads, head_dim, capacity), jnp.bfloat16),
            jax.ShapeDtypeStruct(row_order.shape, jnp.int32),
            jax.ShapeDtypeStruct((tiles * LANES, count * columns), jnp.bfloat16),
        ],
        in_specs=[HBM, HBM, HBM],
        out_specs=[VMEM, VMEM, VMEM, VMEM],
        scratch_shapes=[
            pltpu.VMEM((kv_heads, pieces, KB, head_dim), jnp.bfloat16),
            pltpu.SMEM(row_order.shape, jnp.int32),
            pltpu.SemaphoreType.DMA((3, kv_heads, pieces)),
        ],
        compiler_params=pltpu.CompilerParams(vmem_limit_bytes=8 << 20),
        cost_estimate=cost_of(STAGE_COST),
    )(*in_hbm(cache_keys, cache_values, row_order))

    sent, gathered, start = {}, None, 0
    message_rows = kv_heads * head_dim + 16 * pl.cdiv(3 * kv_heads, 16)
    for steps in plan:
        wide = len(steps) * columns
        shapes = [jax.ShapeDtypeStruct((message_rows, columns), jnp.int16) for _ in steps]
        scores = pltpu.VMEM((kv_heads, capacity, wide), jnp.float32)
        params = pltpu.CompilerParams(vmem_limit_bytes=16 << 20)
        cost = cost_of(OWN_COST if 0 in steps else ATTEND_COST)
        if gathered is None:
            asked, counts, *parts = pl.pallas_call(
                functools.partial(
                    first_kernel, count=count, plan=plan, rows=rows, group=group, scaling=scaling
                ),
                out_shape=[
                    jax.ShapeDtypeStruct((kv_heads, count * columns, head_dim), jnp.bfloat16),
                    jax.ShapeDtypeStruct((8, count * columns), jnp.int32),
                    *shapes,
                ],
                in_specs=[SMEM, VMEM, VMEM, VMEM] + [VMEM] * count,
                out_specs=[VMEM] * (2 + len(steps)),
                scratch_shapes=[pltpu.VMEM((count, body, head_dim), jnp.bfloat16), scores],
                compiler_params=params,
                cost_estimate=cost,
            )(
                order, staged_keys, staged_values, spread,
                *[arrived[s] if s else packed for s in first_order(count)],
            )
            gathered = (asked, counts)
        else:
            parts = pl.pallas_call(
                functools.partial(next_kernel, start=start, scaling=scaling),
                out_shape=shapes,
                in_specs=[VMEM, VMEM, VMEM, VMEM],
                out_specs=[VMEM] * len(steps),
                scratch_shapes=[scores],
                compiler_params=params,
                cost_estimate=cost,
            )(staged_keys, staged_values, *gathered)
        start += wide
        for step, part in zip(steps, parts):
            sent[step] = part if step == 0 else lax.ppermute(part, "blk", shift_pairs(count, step))

    state = []
    joins = join_plan(plan)
    for number, steps in enumerate(joins):
        last = number == len(joins) - 1
        shape = (
            jax.ShapeDtypeStruct((1, rows, heads, head_dim), jnp.bfloat16)
            if last
            else [
                jax.ShapeDtypeStruct((kv_heads, head_dim, columns), jnp.float32),
                jax.ShapeDtypeStruct((kv_heads, 8, columns), jnp.float32),
            ]
        )
        state = pl.pallas_call(
            functools.partial(
                settle_kernel, messages=len(steps), first=not state, last=last,
                kv_heads=kv_heads, width=head_dim, group=group,
            ),
            out_shape=shape,
            in_specs=[VMEM] * (len(steps) + len(state)),
            out_specs=VMEM if last else [VMEM, VMEM],
            compiler_params=pltpu.CompilerParams(vmem_limit_bytes=8 << 20),
            cost_estimate=cost_of(JOIN_COST),
        )(*[sent[step] for step in steps], *state)
    return state


def solution(mesh):
    placed = (
        P(("groups", "beam"), "blk", "heads", None),
        P(("groups", "beam"), "blk"),
        P(("groups", "beam"), None),
        P(("groups", "blk")),
        P(("groups", "blk"), "heads", None, None),
        P(("groups", "blk"), "heads", None, None),
    )
    return jax.shard_map(
        per_device,
        mesh=mesh,
        in_specs=placed,
        out_specs=P(("groups", "beam"), "blk", "heads", None),
        check_vma=False,
    )
```

time: 33.2 us -> 24.1 us (0.73)
  waiting for transfers between devices: 10.6 us -> 4.5 us
  local copies, waits for them, and re-layouts: 4.21 us -> 0 us
  starting transfers between devices: 10 us -> 11.8 us
  Pallas kernels: 7.28 us -> 6.85 us
    ppermute x6, waiting for transfers between devices: 10.6 us -> 4.5 us  [the longest x3 2.64 us: per_device(): lax.ppermute(part, 'blk', shift_pairs(count, step))]
    unnamed x16 -> x0, local copies, waits for them, and re-layouts: 4.21 us -> none
    ppermute x6, starting transfers between devices: 10 us -> 11.8 us  [the longest x3 7.01 us: per_device(): lax.ppermute(packed, 'blk', shift_pairs(count, step))]
    pallas_call x1, Pallas kernels: 1.49 us -> 0.89 us  [per_device(): pl.pallas_call(functools.partial(pack_kernel, tiles=tiles), out_shape=jax...]
    pallas_call x2 -> x8, Pallas kernels: 5.78 us -> 5.96 us  [the longest x3 2.13 us: per_device(): pl.pallas_call(functools.partial(next_kernel, start=start, scaling=scalin...]
  transfers between devices with their start and end apart: 6 -> 6, of which waited for: 5 -> 4; matrix products, arithmetic and copies ran while one was open for 0% -> 0% of each run, Pallas kernels for 0% -> 16%
where the time goes in v2:
time: 24.1 us; the launch traced here: 23.9 us
  starting transfers between devices  11.8 us (49%)
  Pallas kernels  6.85 us (28%)
  waiting for transfers between devices  4.5 us (19%)
  between operations  0.73 us (3%)
    ppermute x3, starting transfers between devices, per_device(): lax.ppermute(packed, 'blk', shift_pairs(count, step))  7.01 us
    ppermute x3, starting transfers between devices, per_device(): lax.ppermute(part, 'blk', shift_pairs(count, step))  4.78 us
    ppermute x3, waiting for transfers between devices, per_device(): lax.ppermute(part, 'blk', shift_pairs(count, step))  2.64 us
    pallas_call x3, Pallas kernels, per_device(): pl.pallas_call(functools.partial(next_kernel, start=start, scaling=scalin...  2.13 us
    ppermute x3, waiting for transfers between devices, per_device(): lax.ppermute(packed, 'blk', shift_pairs(count, step))  1.86 us
    pallas_call x1, Pallas kernels, per_device(): pl.pallas_call(functools.partial(stage_kernel, count=count, plan=plan, ro...  1.66 us
    pallas_call x1, Pallas kernels, per_device(): pl.pallas_call(functools.partial(first_kernel, count=count, plan=plan, ro...  1.34 us
    pallas_call x1, Pallas kernels, per_device(): pl.pallas_call(functools.partial(pack_kernel, tiles=tiles), out_shape=jax...  0.89 us
  transfers between devices with their start and end apart: 6, of which 4 were waited for; matrix products, arithmetic and copies ran while one was open for 0% of the time, Pallas kernels for 16%

profile of v2, /device:TPU:0, one launch (start us, length us, event | category | flops | bytes accessed | tf_op | source)
XLA Modules:
  0.0 23.9 jit_solution(7431706162382105697)
XLA Ops:
  0.7 0.9 %shard_map.65.refs_4_ = bf16[272,128]{1,0:T(8,128)(2,1)S(1)} custom-call(s32[1]{0:T(128)S(6)} %copy.7.lengths_ref, s32[1,8]{1,0:T(1,128)} %positions_ref.1, bf16[1,8,32,128]{3,2,1,0:T(8,128)(2,1)} %queries_ref.1), custom_call_target="tpu_custom_call" | custom-call | tf_op jit(solution)/shard_map/pallas_call | solution.py:284
  1.6 3.1 %collective-permute-start.2 = (bf16[272,128]{1,0:T(8,128)(2,1)S(1)}, bf16[272,128]{1,0:T(8,128)(2,1)S(1)}, u32[]{:S(2)}, u32[]{:S(2)}) collective-permute-start(bf16[272,128]{1,0:T(8,128)(2,1)S(1)} %shard_map.65.refs_4_), channel_id=1, source_target_pairs={{0,4},{4,8},{8,12},{12,0},{1,5},{5,9},{9,13},{13,1},{2,6},{6,10},{... | collective-permute-start | bytes 208904 | tf_op jit(solution)/shard_map/ppermute | solution.py:296
  4.6 2.6 %collective-permute-start.1 = (bf16[272,128]{1,0:T(8,128)(2,1)S(1)}, bf16[272,128]{1,0:T(8,128)(2,1)S(1)}, u32[]{:S(2)}, u32[]{:S(2)}) collective-permute-start(bf16[272,128]{1,0:T(8,128)(2,1)S(1)} %shard_map.65.refs_4_), channel_id=1, source_target_pairs={{0,8},{4,12},{8,0},{12,4},{1,9},{5,13},{9,1},{13,5},{2,10},{6,14},... | collective-permute-start | bytes 208904 | tf_op jit(solution)/shard_map/ppermute | solution.py:296
  7.2 1.3 %collective-permute-start = (bf16[272,128]{1,0:T(8,128)(2,1)S(1)}, bf16[272,128]{1,0:T(8,128)(2,1)S(1)}, u32[]{:S(2)}, u32[]{:S(2)}) collective-permute-start(bf16[272,128]{1,0:T(8,128)(2,1)S(1)} %shard_map.65.refs_4_), channel_id=1, source_target_pairs={{0,12},{4,0},{8,4},{12,8},{1,13},{5,1},{9,5},{13,9},{2,14},{6,2},{... | collective-permute-start | bytes 208904 | tf_op jit(solution)/shard_map/ppermute | solution.py:296
  8.6 1.7 %shard_map.64 = (bf16[2,1024,128]{2,1,0:T(8,128)(2,1)S(1)}, bf16[2,128,1024]{2,1,0:T(8,128)(2,1)S(1)}, s32[1,32]{1,0:T(1,128)S(1)}, bf16[128,512]{1,0:T(8,128)(2,1)S(1)}) custom-call(bf16[1,2,1024,128]{3,2,1,0:T(8,128)(2,1)} %refs_0_.1, bf16[1,2,1024,128]{3,2,1,0:T(8,128)(2,1)} %refs_1_.1, s32[1,32]{1,0:T(1,128)} %refs_2_.1), custom_call_target="tpu_custom_call" | custom-call | flops 16777216 | bytes 1 | tf_op jit(solution)/shard_map/pallas_call | solution.py:301
  10.2 0.0 collective-permute-done.2.refs_7_
  10.2 1.7 %collective-permute-done.1.refs_6_ = bf16[272,128]{1,0:T(8,128)(2,1)S(1)} collective-permute-done((bf16[272,128]{1,0:T(8,128)(2,1)S(1)}, bf16[272,128]{1,0:T(8,128)(2,1)S(1)}, u32[]{:S(2)}, u32[]{:S(2)}) %collective-permute-start.1) | collective-permute-done | bytes 69664 | tf_op jit(solution)/shard_map/ppermute | solution.py:296
  11.9 0.2 collective-permute-done.refs_5_
  12.1 1.3 %shard_map.66 = (bf16[2,512,128]{2,1,0:T(8,128)(2,1)S(1)}, s32[8,512]{1,0:T(8,128)S(1)}, s16[272,128]{1,0:T(8,128)(2,1)S(1)}) custom-call(s32[1,32]{1,0:T(1,128)S(1)} %get-tuple-element.18.refs_0_, bf16[2,1024,128]{2,1,0:T(8,128)(2,1)S(1)} %get-tuple-element.16.refs_1_.refs_0_, bf16[2,128,1024]{2,1,0:T(8,128)(2,1)S(1)} %get-tuple-element.17.refs_2_.refs_1_, ...), custom_call_target="tpu_custom_call" | custom-call | flops 1 | bytes 1 | tf_op jit(solution)/shard_map/pallas_call | solution.py:329
  13.5 0.9 %collective-permute-start.5 = (s16[272,128]{1,0:T(8,128)(2,1)S(1)}, s16[272,128]{1,0:T(8,128)(2,1)S(1)}, u32[]{:S(2)}, u32[]{:S(2)}) collective-permute-start(s16[272,128]{1,0:T(8,128)(2,1)S(1)} %get-tuple-element.22), channel_id=1, source_target_pairs={{0,8},{4,12},{8,0},{12,4},{1,9},{5,13},{9,1},{13,5},{2,10},{6,14},... | collective-permute-start | bytes 208904 | tf_op jit(solution)/shard_map/ppermute | solution.py:360
  14.3 0.7 %shard_map.68 = s16[272,128]{1,0:T(8,128)(2,1)S(1)} custom-call(bf16[2,1024,128]{2,1,0:T(8,128)(2,1)S(1)} %get-tuple-element.16.refs_1_.refs_0_, bf16[2,128,1024]{2,1,0:T(8,128)(2,1)S(1)} %get-tuple-element.17.refs_2_.refs_1_, bf16[2,512,128]{2,1,0:T(8,128)(2,1)S(1)} %get-tuple-element.20.refs_2_, s32[8,512]{1,0:T(8,128)S(1)} %get-tuple-element.21.refs_3_), custom_call_target="tpu_custom_call" | custom-call | flops 1 | bytes 1 | tf_op jit(solution)/shard_map/pallas_call | solution.py:349
  15.0 3.0 %collective-permute-start.4 = (s16[272,128]{1,0:T(8,128)(2,1)S(1)}, s16[272,128]{1,0:T(8,128)(2,1)S(1)}, u32[]{:S(2)}, u32[]{:S(2)}) collective-permute-start(s16[272,128]{1,0:T(8,128)(2,1)S(1)} %shard_map.68), channel_id=1, source_target_pairs={{0,4},{4,8},{8,12},{12,0},{1,5},{5,9},{9,13},{13,1},{2,6},{6,10},{... | collective-permute-start | bytes 208904 | tf_op jit(solution)/shard_map/ppermute | solution.py:360
  18.0 0.7 %shard_map.67 = s16[272,128]{1,0:T(8,128)(2,1)S(1)} custom-call(bf16[2,1024,128]{2,1,0:T(8,128)(2,1)S(1)} %get-tuple-element.16.refs_1_.refs_0_, bf16[2,128,1024]{2,1,0:T(8,128)(2,1)S(1)} %get-tuple-element.17.refs_2_.refs_1_, bf16[2,512,128]{2,1,0:T(8,128)(2,1)S(1)} %get-tuple-element.20.refs_2_, s32[8,512]{1,0:T(8,128)S(1)} %get-tuple-element.21.refs_3_), custom_call_target="tpu_custom_call" | custom-call | flops 1 | bytes 1 | tf_op jit(solution)/shard_map/pallas_call | solution.py:349
  18.8 0.9 %collective-permute-start.3 = (s16[272,128]{1,0:T(8,128)(2,1)S(1)}, s16[272,128]{1,0:T(8,128)(2,1)S(1)}, u32[]{:S(2)}, u32[]{:S(2)}) collective-permute-start(s16[272,128]{1,0:T(8,128)(2,1)S(1)} %shard_map.67), channel_id=1, source_target_pairs={{0,12},{4,0},{8,4},{12,8},{1,13},{5,1},{9,5},{13,9},{2,14},{6,2},{... | collective-permute-start | bytes 208904 | tf_op jit(solution)/shard_map/ppermute | solution.py:360
  19.7 0.7 %shard_map.69.refs_0_ = s16[272,128]{1,0:T(8,128)(2,1)S(1)} custom-call(bf16[2,1024,128]{2,1,0:T(8,128)(2,1)S(1)} %get-tuple-element.16.refs_1_.refs_0_, bf16[2,128,1024]{2,1,0:T(8,128)(2,1)S(1)} %get-tuple-element.17.refs_2_.refs_1_, bf16[2,512,128]{2,1,0:T(8,128)(2,1)S(1)} %get-tuple-element.20.refs_2_, s32[8,512]{1,0:T(8,128)S(1)} %get-tuple-element.21.refs_3_), custom_call_target="tpu_custom_call" | custom-call | flops 1 | bytes 1 | tf_op jit(solution)/shard_map/pallas_call | solution.py:349
  20.4 1.6 %collective-permute-done.5.refs_1_ = s16[272,128]{1,0:T(8,128)(2,1)S(1)} collective-permute-done((s16[272,128]{1,0:T(8,128)(2,1)S(1)}, s16[272,128]{1,0:T(8,128)(2,1)S(1)}, u32[]{:S(2)}, u32[]{:S(2)}) %collective-permute-start.5) | collective-permute-done | bytes 69664 | tf_op jit(solution)/shard_map/ppermute | solution.py:360
  22.0 0.0 collective-permute-done.4.refs_0_
  22.1 1.1 %collective-permute-done.3.refs_0_ = s16[272,128]{1,0:T(8,128)(2,1)S(1)} collective-permute-done((s16[272,128]{1,0:T(8,128)(2,1)S(1)}, s16[272,128]{1,0:T(8,128)(2,1)S(1)}, u32[]{:S(2)}, u32[]{:S(2)}) %collective-permute-start.3) | collective-permute-done | bytes 69664 | tf_op jit(solution)/shard_map/ppermute | solution.py:360
  23.1 0.8 %shard_map.72 = bf16[1,8,32,128]{3,2,1,0:T(8,128)(2,1)} custom-call(s16[272,128]{1,0:T(8,128)(2,1)S(1)} %collective-permute-done.3.refs_0_, f32[2,128,128]{2,1,0:T(8,128)S(1)} %get-tuple-element.25.refs_1_, f32[2,8,128]{2,1,0:T(8,128)S(1)} %get-tuple-element.26.refs_2_), custom_call_target="tpu_custom_call" | custom-call | flops 1 | bytes 1 | tf_op jit(solution)/shard_map/pallas_call | solution.py:374
  (2 shorter events, 0.1 us)
Async XLA Ops:
  1.6 8.7 %collective-permute-start.2 = (bf16[272,128]{1,0:T(8,128)(2,1)S(1)}, bf16[272,128]{1,0:T(8,128)(2,1)S(1)}, u32[]{:S(2)}, u32[]{:S(2)}) collective-permute-start(bf16[272,128]{1,0:T(8,128)(2,1)S(1)} %shard_map.65.refs_4_), channel_id=1, source_target_pairs={{0,4},{4,8},{8,12},{12,0},{1,5},{5,9},{9,13},{13,1},{2,6},{6,10},{... | collective-permute-start | bytes 208904 | tf_op jit(solution)/shard_map/ppermute | solution.py:296
  4.6 7.3 %collective-permute-start.1 = (bf16[272,128]{1,0:T(8,128)(2,1)S(1)}, bf16[272,128]{1,0:T(8,128)(2,1)S(1)}, u32[]{:S(2)}, u32[]{:S(2)}) collective-permute-start(bf16[272,128]{1,0:T(8,128)(2,1)S(1)} %shard_map.65.refs_4_), channel_id=1, source_target_pairs={{0,8},{4,12},{8,0},{12,4},{1,9},{5,13},{9,1},{13,5},{2,10},{6,14},... | collective-permute-start | bytes 208904 | tf_op jit(solution)/shard_map/ppermute | solution.py:296
  7.2 4.9 %collective-permute-start = (bf16[272,128]{1,0:T(8,128)(2,1)S(1)}, bf16[272,128]{1,0:T(8,128)(2,1)S(1)}, u32[]{:S(2)}, u32[]{:S(2)}) collective-permute-start(bf16[272,128]{1,0:T(8,128)(2,1)S(1)} %shard_map.65.refs_4_), channel_id=1, source_target_pairs={{0,12},{4,0},{8,4},{12,8},{1,13},{5,1},{9,5},{13,9},{2,14},{6,2},{... | collective-permute-start | bytes 208904 | tf_op jit(solution)/shard_map/ppermute | solution.py:296
  13.5 8.5 %collective-permute-start.5 = (s16[272,128]{1,0:T(8,128)(2,1)S(1)}, s16[272,128]{1,0:T(8,128)(2,1)S(1)}, u32[]{:S(2)}, u32[]{:S(2)}) collective-permute-start(s16[272,128]{1,0:T(8,128)(2,1)S(1)} %get-tuple-element.22), channel_id=1, source_target_pairs={{0,8},{4,12},{8,0},{12,4},{1,9},{5,13},{9,1},{13,5},{2,10},{6,14},... | collective-permute-start | bytes 208904 | tf_op jit(solution)/shard_map/ppermute | solution.py:360
  15.0 7.0 %collective-permute-start.4 = (s16[272,128]{1,0:T(8,128)(2,1)S(1)}, s16[272,128]{1,0:T(8,128)(2,1)S(1)}, u32[]{:S(2)}, u32[]{:S(2)}) collective-permute-start(s16[272,128]{1,0:T(8,128)(2,1)S(1)} %shard_map.68), channel_id=1, source_target_pairs={{0,4},{4,8},{8,12},{12,0},{1,5},{5,9},{9,13},{13,1},{2,6},{6,10},{... | collective-permute-start | bytes 208904 | tf_op jit(solution)/shard_map/ppermute | solution.py:360
  18.8 4.4 %collective-permute-start.3 = (s16[272,128]{1,0:T(8,128)(2,1)S(1)}, s16[272,128]{1,0:T(8,128)(2,1)S(1)}, u32[]{:S(2)}, u32[]{:S(2)}) collective-permute-start(s16[272,128]{1,0:T(8,128)(2,1)S(1)} %shard_map.67), channel_id=1, source_target_pairs={{0,12},{4,0},{8,4},{12,8},{1,13},{5,1},{9,5},{13,9},{2,14},{6,2},{... | collective-permute-start | bytes 208904 | tf_op jit(solution)/shard_map/ppermute | solution.py:360

commit v3 on v2

--- a/solution.py
+++ b/solution.py
@@ -26,11 +26,11 @@
     return [(i, (i + step) % count) for i in range(count)]
 
 
-def first_source(me, count, step):
+def shift_source(me, count, step):
     return lax.rem(me - step + count, count)
 
 
-def second_target(me, count, step):
+def shift_target(me, count, step):
     return lax.rem(me + step, count)
 
 
@@ -106,7 +106,7 @@
     for at, step in enumerate(sum(plan, [])):
         chosen = jnp.zeros((1, columns), jnp.int32)
         for i in range(rows):
-            chosen = jnp.where(lane_row == i, order[0, second_target(me, count, step) * rows + i], chosen)
+            chosen = jnp.where(lane_row == i, order[0, shift_target(me, count, step) * rows + i], chosen)
         spread = jnp.where(spread_row == chosen, 1.0, 0.0).astype(jnp.bfloat16)
         spread_ref[:, at * columns : (at + 1) * columns] = spread
     for kv in range(kv_heads):
@@ -174,7 +174,7 @@
     body = held.shape[1]
     tiles = spread_ref.shape[0] // LANES
     for step, ref in zip(first_order(count), message_refs):
-        held[first_source(me, count, step)] = ref[:body]
+        held[shift_source(me, count, step)] = ref[:body]
     offset = jnp.zeros((1, 1), jnp.float32)
     own_length = jnp.zeros((1, 1), jnp.float32)
     pos = []
@@ -197,7 +197,7 @@
     asked = [[] for _ in range(kv_heads)]
     for at, step in enumerate(sum(plan, [])):
         for i in range(rows):
-            row = order_ref[0, second_target(me, count, step) * rows + i]
+            row = order_ref[0, shift_target(me, count, step) * rows + i]
             source = lax.div(row, rows)
             inner = row - source * rows
             for kv in range(kv_heads):
@@ -259,13 +259,17 @@
 
 
 def exchange_plan(count):
-    later = sorted(range(1, count), key=lambda step: (abs(2 * step - count), step)) + [0]
+    later = sorted(range(1, count), key=lambda step: (abs(2 * step - count), step))
     chunk = pl.cdiv(count, 4)
-    return [later[i : i + chunk] for i in range(0, count, chunk)]
+    rest = later[chunk:]
+    pairs = [rest[i : i + 2 * chunk] for i in range(0, len(rest), 2 * chunk)]
+    return [later[:chunk], *pairs, [0]]
 
 
 def join_plan(plan):
-    return [plan[-1] + plan[0]] + plan[1:-1]
+    chunk = len(plan[0])
+    rest = sum(plan[1:-1], [])
+    return [plan[-1] + plan[0]] + [rest[i : i + chunk] for i in range(0, len(rest), chunk)]
 
 
 def cost_of(flops):
@@ -303,11 +307,11 @@
         out_shape=[
             jax.ShapeDtypeStruct((kv_heads, capacity, head_dim), jnp.bfloat16),
             jax.ShapeDtypeStruct((kv_heads, head_dim, capacity), jnp.bfloat16),
-            jax.ShapeDtypeStruct(row_order.shape, jnp.int32),
+            pltpu.SMEM(row_order.shape, jnp.int32),
             jax.ShapeDtypeStruct((tiles * LANES, count * columns), jnp.bfloat16),
         ],
         in_specs=[HBM, HBM, HBM],
-        out_specs=[VMEM, VMEM, VMEM, VMEM],
+        out_specs=[VMEM, VMEM, SMEM, VMEM],
         scratch_shapes=[
             pltpu.VMEM((kv_heads, pieces, KB, head_dim), jnp.bfloat16),
             pltpu.SMEM(row_order.shape, jnp.int32),

time: 24.1 us -> 23.3 us (0.967)
  Pallas kernels: 6.85 us -> 5.91 us
    pallas_call x1, Pallas kernels: 1.34 us -> 0.79 us  [per_device(): pl.pallas_call(functools.partial(first_kernel, count=count, plan=plan, ro...]
    pallas_call x3 -> x2, Pallas kernels: 2.13 us -> 1.75 us  [per_device(): pl.pallas_call(functools.partial(next_kernel, start=start, scaling=scalin...]
  transfers between devices with their start and end apart: 6 -> 6, of which waited for: 4 -> 5; matrix products, arithmetic and copies ran while one was open for 0% -> 0% of each run, Pallas kernels for 16% -> 15%
where the time goes in v3:
time: 23.3 us; the launch traced here: 23.1 us
  starting transfers between devices  11.8 us (51%)
  Pallas kernels  5.91 us (25%)
  waiting for transfers between devices  4.68 us (20%)
  between operations  0.71 us (3%)
    ppermute x3, starting transfers between devices, per_device(): lax.ppermute(packed, 'blk', shift_pairs(count, step))  7.01 us
    ppermute x3, starting transfers between devices, per_device(): lax.ppermute(part, 'blk', shift_pairs(count, step))  4.74 us
    ppermute x3, waiting for transfers between devices, per_device(): lax.ppermute(part, 'blk', shift_pairs(count, step))  2.8 us
    ppermute x3, waiting for transfers between devices, per_device(): lax.ppermute(packed, 'blk', shift_pairs(count, step))  1.88 us
    pallas_call x2, Pallas kernels, per_device(): pl.pallas_call(functools.partial(next_kernel, start=start, scaling=scalin...  1.75 us
    pallas_call x1, Pallas kernels, per_device(): pl.pallas_call(functools.partial(stage_kernel, count=count, plan=plan, ro...  1.64 us
    pallas_call x1, Pallas kernels, per_device(): pl.pallas_call(functools.partial(pack_kernel, tiles=tiles), out_shape=jax...  0.89 us
    pallas_call x3, Pallas kernels, per_device(): pl.pallas_call(functools.partial(settle_kernel, messages=len(steps), firs...  0.83 us
  transfers between devices with their start and end apart: 6, of which 5 were waited for; matrix products, arithmetic and copies ran while one was open for 0% of the time, Pallas kernels for 15%

profile of v3, /device:TPU:0, one launch (start us, length us, event | category | flops | bytes accessed | tf_op | source)
XLA Modules:
  0.0 23.1 jit_solution(14930339100409933038)
XLA Ops:
  0.7 0.9 %shard_map.65.refs_4_ = bf16[272,128]{1,0:T(8,128)(2,1)S(1)} custom-call(s32[1]{0:T(128)S(6)} %copy.7.lengths_ref, s32[1,8]{1,0:T(1,128)} %positions_ref.1, bf16[1,8,32,128]{3,2,1,0:T(8,128)(2,1)} %queries_ref.1), custom_call_target="tpu_custom_call" | custom-call | tf_op jit(solution)/shard_map/pallas_call | solution.py:288
  1.6 3.1 %collective-permute-start.2 = (bf16[272,128]{1,0:T(8,128)(2,1)S(1)}, bf16[272,128]{1,0:T(8,128)(2,1)S(1)}, u32[]{:S(2)}, u32[]{:S(2)}) collective-permute-start(bf16[272,128]{1,0:T(8,128)(2,1)S(1)} %shard_map.65.refs_4_), channel_id=1, source_target_pairs={{0,4},{4,8},{8,12},{12,0},{1,5},{5,9},{9,13},{13,1},{2,6},{6,10},{... | collective-permute-start | bytes 208904 | tf_op jit(solution)/shard_map/ppermute | solution.py:300
  4.6 2.6 %collective-permute-start.1 = (bf16[272,128]{1,0:T(8,128)(2,1)S(1)}, bf16[272,128]{1,0:T(8,128)(2,1)S(1)}, u32[]{:S(2)}, u32[]{:S(2)}) collective-permute-start(bf16[272,128]{1,0:T(8,128)(2,1)S(1)} %shard_map.65.refs_4_), channel_id=1, source_target_pairs={{0,8},{4,12},{8,0},{12,4},{1,9},{5,13},{9,1},{13,5},{2,10},{6,14},... | collective-permute-start | bytes 208904 | tf_op jit(solution)/shard_map/ppermute | solution.py:300
  7.2 1.3 %collective-permute-start = (bf16[272,128]{1,0:T(8,128)(2,1)S(1)}, bf16[272,128]{1,0:T(8,128)(2,1)S(1)}, u32[]{:S(2)}, u32[]{:S(2)}) collective-permute-start(bf16[272,128]{1,0:T(8,128)(2,1)S(1)} %shard_map.65.refs_4_), channel_id=1, source_target_pairs={{0,12},{4,0},{8,4},{12,8},{1,13},{5,1},{9,5},{13,9},{2,14},{6,2},{... | collective-permute-start | bytes 208904 | tf_op jit(solution)/shard_map/ppermute | solution.py:300
  8.6 1.6 %shard_map.64 = (bf16[2,1024,128]{2,1,0:T(8,128)(2,1)S(1)}, bf16[2,128,1024]{2,1,0:T(8,128)(2,1)S(1)}, s32[1,32]{1,0:T(1,128)S(4)}, bf16[128,512]{1,0:T(8,128)(2,1)S(1)}) custom-call(bf16[1,2,1024,128]{3,2,1,0:T(8,128)(2,1)} %refs_0_.1, bf16[1,2,1024,128]{3,2,1,0:T(8,128)(2,1)} %refs_1_.1, s32[1,32]{1,0:T(1,128)} %refs_2_.1), custom_call_target="tpu_custom_call" | custom-call | flops 16777216 | bytes 1 | tf_op jit(solution)/shard_map/pallas_call | solution.py:305
  10.2 0.0 collective-permute-done.2.refs_7_
  10.2 1.7 %collective-permute-done.1.refs_6_ = bf16[272,128]{1,0:T(8,128)(2,1)S(1)} collective-permute-done((bf16[272,128]{1,0:T(8,128)(2,1)S(1)}, bf16[272,128]{1,0:T(8,128)(2,1)S(1)}, u32[]{:S(2)}, u32[]{:S(2)}) %collective-permute-start.1) | collective-permute-done | bytes 69664 | tf_op jit(solution)/shard_map/ppermute | solution.py:300
  11.9 0.2 collective-permute-done.refs_5_
  12.1 0.8 %shard_map.66 = (bf16[2,512,128]{2,1,0:T(8,128)(2,1)S(1)}, s32[8,512]{1,0:T(8,128)S(1)}, s16[272,128]{1,0:T(8,128)(2,1)S(1)}) custom-call(s32[1,32]{1,0:T(1,128)S(4)} %get-tuple-element.20.refs_0_, bf16[2,1024,128]{2,1,0:T(8,128)(2,1)S(1)} %get-tuple-element.18.refs_1_.refs_0_, bf16[2,128,1024]{2,1,0:T(8,128)(2,1)S(1)} %get-tuple-element.19.refs_2_.refs_1_, ...), custom_call_target="tpu_custom_call" | custom-call | flops 1 | bytes 1 | tf_op jit(solution)/shard_map/pallas_call | solution.py:333
  12.9 0.9 %collective-permute-start.5 = (s16[272,128]{1,0:T(8,128)(2,1)S(1)}, s16[272,128]{1,0:T(8,128)(2,1)S(1)}, u32[]{:S(2)}, u32[]{:S(2)}) collective-permute-start(s16[272,128]{1,0:T(8,128)(2,1)S(1)} %get-tuple-element.26), channel_id=1, source_target_pairs={{0,8},{4,12},{8,0},{12,4},{1,9},{5,13},{9,1},{13,5},{2,10},{6,14},... | collective-permute-start | bytes 208904 | tf_op jit(solution)/shard_map/ppermute | solution.py:364
  13.8 1.0 %shard_map.67 = (s16[272,128]{1,0:T(8,128)(2,1)S(1)}, s16[272,128]{1,0:T(8,128)(2,1)S(1)}) custom-call(bf16[2,1024,128]{2,1,0:T(8,128)(2,1)S(1)} %get-tuple-element.18.refs_1_.refs_0_, bf16[2,128,1024]{2,1,0:T(8,128)(2,1)S(1)} %get-tuple-element.19.refs_2_.refs_1_, bf16[2,512,128]{2,1,0:T(8,128)(2,1)S(1)} %get-tuple-element.22.refs_2_, ...), custom_call_target="tpu_custom_call" | custom-call | flops 1 | bytes 1 | tf_op jit(solution)/shard_map/pallas_call | solution.py:353
  14.8 3.0 %collective-permute-start.4 = (s16[272,128]{1,0:T(8,128)(2,1)S(1)}, s16[272,128]{1,0:T(8,128)(2,1)S(1)}, u32[]{:S(2)}, u32[]{:S(2)}) collective-permute-start(s16[272,128]{1,0:T(8,128)(2,1)S(1)} %get-tuple-element.25), channel_id=1, source_target_pairs={{0,4},{4,8},{8,12},{12,0},{1,5},{5,9},{9,13},{13,1},{2,6},{6,10},{... | collective-permute-start | bytes 208904 | tf_op jit(solution)/shard_map/ppermute | solution.py:364
  17.8 0.9 %collective-permute-start.3 = (s16[272,128]{1,0:T(8,128)(2,1)S(1)}, s16[272,128]{1,0:T(8,128)(2,1)S(1)}, u32[]{:S(2)}, u32[]{:S(2)}) collective-permute-start(s16[272,128]{1,0:T(8,128)(2,1)S(1)} %get-tuple-element.24), channel_id=1, source_target_pairs={{0,12},{4,0},{8,4},{12,8},{1,13},{5,1},{9,5},{13,9},{2,14},{6,2},{... | collective-permute-start | bytes 208904 | tf_op jit(solution)/shard_map/ppermute | solution.py:364
  18.7 0.7 %shard_map.68.refs_0_ = s16[272,128]{1,0:T(8,128)(2,1)S(1)} custom-call(bf16[2,1024,128]{2,1,0:T(8,128)(2,1)S(1)} %get-tuple-element.18.refs_1_.refs_0_, bf16[2,128,1024]{2,1,0:T(8,128)(2,1)S(1)} %get-tuple-element.19.refs_2_.refs_1_, bf16[2,512,128]{2,1,0:T(8,128)(2,1)S(1)} %get-tuple-element.22.refs_2_, s32[8,512]{1,0:T(8,128)S(1)} %get-tuple-element.23.refs_3_), custom_call_target="tpu_custom_call" | custom-call | flops 1 | bytes 1 | tf_op jit(solution)/shard_map/pallas_call | solution.py:353
  19.4 1.6 %collective-permute-done.5.refs_1_ = s16[272,128]{1,0:T(8,128)(2,1)S(1)} collective-permute-done((s16[272,128]{1,0:T(8,128)(2,1)S(1)}, s16[272,128]{1,0:T(8,128)(2,1)S(1)}, u32[]{:S(2)}, u32[]{:S(2)}) %collective-permute-start.5) | collective-permute-done | bytes 69664 | tf_op jit(solution)/shard_map/ppermute | solution.py:364
  21.1 0.6 %collective-permute-done.4.refs_0_ = s16[272,128]{1,0:T(8,128)(2,1)S(1)} collective-permute-done((s16[272,128]{1,0:T(8,128)(2,1)S(1)}, s16[272,128]{1,0:T(8,128)(2,1)S(1)}, u32[]{:S(2)}, u32[]{:S(2)}) %collective-permute-start.4) | collective-permute-done | bytes 69664 | tf_op jit(solution)/shard_map/ppermute | solution.py:364
  21.8 0.5 %collective-permute-done.3.refs_0_ = s16[272,128]{1,0:T(8,128)(2,1)S(1)} collective-permute-done((s16[272,128]{1,0:T(8,128)(2,1)S(1)}, s16[272,128]{1,0:T(8,128)(2,1)S(1)}, u32[]{:S(2)}, u32[]{:S(2)}) %collective-permute-start.3) | collective-permute-done | bytes 69664 | tf_op jit(solution)/shard_map/ppermute | solution.py:364
  22.3 0.8 %shard_map.71 = bf16[1,8,32,128]{3,2,1,0:T(8,128)(2,1)} custom-call(s16[272,128]{1,0:T(8,128)(2,1)S(1)} %collective-permute-done.3.refs_0_, f32[2,128,128]{2,1,0:T(8,128)S(1)} %get-tuple-element.29.refs_1_, f32[2,8,128]{2,1,0:T(8,128)S(1)} %get-tuple-element.30.refs_2_), custom_call_target="tpu_custom_call" | custom-call | flops 1 | bytes 1 | tf_op jit(solution)/shard_map/pallas_call | solution.py:378
  (2 shorter events, 0.1 us)
Async XLA Ops:
  1.6 8.7 %collective-permute-start.2 = (bf16[272,128]{1,0:T(8,128)(2,1)S(1)}, bf16[272,128]{1,0:T(8,128)(2,1)S(1)}, u32[]{:S(2)}, u32[]{:S(2)}) collective-permute-start(bf16[272,128]{1,0:T(8,128)(2,1)S(1)} %shard_map.65.refs_4_), channel_id=1, source_target_pairs={{0,4},{4,8},{8,12},{12,0},{1,5},{5,9},{9,13},{13,1},{2,6},{6,10},{... | collective-permute-start | bytes 208904 | tf_op jit(solution)/shard_map/ppermute | solution.py:300
  4.6 7.3 %collective-permute-start.1 = (bf16[272,128]{1,0:T(8,128)(2,1)S(1)}, bf16[272,128]{1,0:T(8,128)(2,1)S(1)}, u32[]{:S(2)}, u32[]{:S(2)}) collective-permute-start(bf16[272,128]{1,0:T(8,128)(2,1)S(1)} %shard_map.65.refs_4_), channel_id=1, source_target_pairs={{0,8},{4,12},{8,0},{12,4},{1,9},{5,13},{9,1},{13,5},{2,10},{6,14},... | collective-permute-start | bytes 208904 | tf_op jit(solution)/shard_map/ppermute | solution.py:300
  7.2 4.9 %collective-permute-start = (bf16[272,128]{1,0:T(8,128)(2,1)S(1)}, bf16[272,128]{1,0:T(8,128)(2,1)S(1)}, u32[]{:S(2)}, u32[]{:S(2)}) collective-permute-start(bf16[272,128]{1,0:T(8,128)(2,1)S(1)} %shard_map.65.refs_4_), channel_id=1, source_target_pairs={{0,12},{4,0},{8,4},{12,8},{1,13},{5,1},{9,5},{13,9},{2,14},{6,2},{... | collective-permute-start | bytes 208904 | tf_op jit(solution)/shard_map/ppermute | solution.py:300
  12.9 8.1 %collective-permute-start.5 = (s16[272,128]{1,0:T(8,128)(2,1)S(1)}, s16[272,128]{1,0:T(8,128)(2,1)S(1)}, u32[]{:S(2)}, u32[]{:S(2)}) collective-permute-start(s16[272,128]{1,0:T(8,128)(2,1)S(1)} %get-tuple-element.26), channel_id=1, source_target_pairs={{0,8},{4,12},{8,0},{12,4},{1,9},{5,13},{9,1},{13,5},{2,10},{6,14},... | collective-permute-start | bytes 208904 | tf_op jit(solution)/shard_map/ppermute | solution.py:364
  14.8 6.9 %collective-permute-start.4 = (s16[272,128]{1,0:T(8,128)(2,1)S(1)}, s16[272,128]{1,0:T(8,128)(2,1)S(1)}, u32[]{:S(2)}, u32[]{:S(2)}) collective-permute-start(s16[272,128]{1,0:T(8,128)(2,1)S(1)} %get-tuple-element.25), channel_id=1, source_target_pairs={{0,4},{4,8},{8,12},{12,0},{1,5},{5,9},{9,13},{13,1},{2,6},{6,10},{... | collective-permute-start | bytes 208904 | tf_op jit(solution)/shard_map/ppermute | solution.py:364
  17.8 4.5 %collective-permute-start.3 = (s16[272,128]{1,0:T(8,128)(2,1)S(1)}, s16[272,128]{1,0:T(8,128)(2,1)S(1)}, u32[]{:S(2)}, u32[]{:S(2)}) collective-permute-start(s16[272,128]{1,0:T(8,128)(2,1)S(1)} %get-tuple-element.24), channel_id=1, source_target_pairs={{0,12},{4,0},{8,4},{12,8},{1,13},{5,1},{9,5},{13,9},{2,14},{6,2},{... | collective-permute-start | bytes 208904 | tf_op jit(solution)/shard_map/ppermute | solution.py:364

commit v4 on v3

--- a/solution.py
+++ b/solution.py
@@ -116,20 +116,20 @@
             copies[0, kv, piece].wait()
 
 
-def attend(keys_ref, values_ref, asked, counts, out_refs, scores, scaling):
-    kv_heads, capacity, wide = scores.shape
+def attend(keys_ref, values_ref, asked, counts, out_refs, scores, scaling, blocks):
+    kv_heads, _, wide = scores.shape
     columns = wide // len(out_refs)
     head_dim = values_ref.shape[1]
     slot = lax.broadcasted_iota(jnp.int32, (KB, wide), 0)
     rate = scaling * math.log2(math.e)
     for kv in range(kv_heads):
-        scores[kv] = lax.dot_general(
-            keys_ref[kv], asked[kv], (((1,), (1,)), ((), ())), preferred_element_type=jnp.float32
+        scores[kv, : blocks * KB] = lax.dot_general(
+            keys_ref[kv, : blocks * KB], asked[kv], (((1,), (1,)), ((), ())), preferred_element_type=jnp.float32
         )
     stats = []
     for kv in range(kv_heads):
         tops, totals, outs = [], [], []
-        for block in range(capacity // KB):
+        for block in range(blocks):
             at = pl.ds(block * KB, KB)
             seen = jnp.where(slot < counts - block * KB, scores[kv, at], MASKED)
             top = jnp.max(seen, axis=0, keepdims=True)
@@ -162,7 +162,25 @@
         ref[kv_heads * head_dim :] = stats[:, at * columns : (at + 1) * columns]
 
 
-def first_kernel(*refs, count, plan, rows, group, scaling):
+def by_live_blocks(lengths_ref, capacity, body):
+    live = lax.div(lengths_ref[0] + (KB - 1), KB)
+    most = capacity // KB
+    live = jnp.minimum(jnp.maximum(live, 1), most)
+    for blocks in range(1, most + 1):
+        pl.when(live == blocks)(functools.partial(body, blocks))
+
+
+def first_kernel(lengths_ref, *refs, count, plan, rows, group, scaling):
+    by_live_blocks(
+        lengths_ref,
+        refs[1].shape[1],
+        lambda blocks: first_body(
+            *refs, count=count, plan=plan, rows=rows, group=group, scaling=scaling, blocks=blocks
+        ),
+    )
+
+
+def first_body(*refs, count, plan, rows, group, scaling, blocks):
     order_ref, keys_ref, values_ref, spread_ref = refs[:4]
     message_refs = refs[4 : 4 + count]
     asked_ref, counts_ref = refs[4 + count : 6 + count]
@@ -207,16 +225,20 @@
                 if at < len(out_refs):
                     asked[kv].append(query)
     asked = [jnp.concatenate(queries, axis=0) for queries in asked]
-    attend(keys_ref, values_ref, asked, counts[:, :wide], out_refs, scores, scaling)
-
-
-def next_kernel(*refs, start, scaling):
+    attend(keys_ref, values_ref, asked, counts[:, :wide], out_refs, scores, scaling, blocks)
+
+
+def next_kernel(lengths_ref, *refs, start, scaling):
     keys_ref, values_ref, asked_ref, counts_ref = refs[:4]
     out_refs, scores = refs[4:-1], refs[-1]
     kv_heads, _, wide = scores.shape
-    asked = [asked_ref[kv, pl.ds(start, wide)] for kv in range(kv_heads)]
-    counts = counts_ref[0:1, start : start + wide]
-    attend(keys_ref, values_ref, asked, counts, out_refs, scores, scaling)
+
+    def body(blocks):
+        asked = [asked_ref[kv, pl.ds(start, wide)] for kv in range(kv_heads)]
+        counts = counts_ref[0:1, start : start + wide]
+        attend(keys_ref, values_ref, asked, counts, out_refs, scores, scaling, blocks)
+
+    by_live_blocks(lengths_ref, keys_ref.shape[1], body)
 
 
 def settle_kernel(*refs, messages, first, last, kv_heads, width, group):
@@ -339,13 +361,13 @@
                     jax.ShapeDtypeStruct((8, count * columns), jnp.int32),
                     *shapes,
                 ],
-                in_specs=[SMEM, VMEM, VMEM, VMEM] + [VMEM] * count,
+                in_specs=[SMEM, SMEM, VMEM, VMEM, VMEM] + [VMEM] * count,
                 out_specs=[VMEM] * (2 + len(steps)),
                 scratch_shapes=[pltpu.VMEM((count, body, head_dim), jnp.bfloat16), scores],
                 compiler_params=params,
                 cost_estimate=cost,
             )(
-                order, staged_keys, staged_values, spread,
+                lengths, order, staged_keys, staged_values, spread,
                 *[arrived[s] if s else packed for s in first_order(count)],
             )
             gathered = (asked, counts)
@@ -353,12 +375,12 @@
             parts = pl.pallas_call(
                 functools.partial(next_kernel, start=start, scaling=scaling),
                 out_shape=shapes,
-                in_specs=[VMEM, VMEM, VMEM, VMEM],
+                in_specs=[SMEM, VMEM, VMEM, VMEM, VMEM],
                 out_specs=[VMEM] * len(steps),
                 scratch_shapes=[scores],
                 compiler_params=params,
                 cost_estimate=cost,
-            )(staged_keys, staged_values, *gathered)
+            )(lengths, staged_keys, staged_values, *gathered)
         start += wide
         for step, part in zip(steps, parts):
             sent[step] = part if step == 0 else lax.ppermute(part, "blk", shift_pairs(count, step))

time: 23.3 us -> 23.2 us (level)
  Pallas kernels: 5.91 us -> 4.92 us
  waiting for transfers between devices: 4.68 us -> 5.26 us
  starting transfers between devices: 11.8 us -> 12.1 us
    pallas_call x2, Pallas kernels: 1.75 us -> 1 us  [per_device(): pl.pallas_call(functools.partial(next_kernel, start=start, scaling=scalin...]
    ppermute x3, waiting for transfers between devices: 2.8 us -> 3.38 us  [per_device(): lax.ppermute(part, 'blk', shift_pairs(count, step))]
    ppermute x3, starting transfers between devices: 4.74 us -> 5.04 us  [per_device(): lax.ppermute(part, 'blk', shift_pairs(count, step))]
    pallas_call x1, Pallas kernels: 0.79 us -> 0.56 us  [per_device(): pl.pallas_call(functools.partial(first_kernel, count=count, plan=plan, ro...]
  transfers between devices with their start and end apart: 6 -> 6, of which waited for: 5 -> 5; matrix products, arithmetic and copies ran while one was open for 0% -> 0% of each run, Pallas kernels for 15% -> 12%
where the time goes in v4:
time: 23.2 us; the launch traced here: 22.9 us
  starting transfers between devices  12.1 us (52%)
  waiting for transfers between devices  5.26 us (23%)
  Pallas kernels  4.92 us (21%)
  between operations  0.71 us (3%)
    ppermute x3, starting transfers between devices, per_device(): lax.ppermute(packed, 'blk', shift_pairs(count, step))  7.01 us
    ppermute x3, starting transfers between devices, per_device(): lax.ppermute(part, 'blk', shift_pairs(count, step))  5.04 us
    ppermute x3, waiting for transfers between devices, per_device(): lax.ppermute(part, 'blk', shift_pairs(count, step))  3.38 us
    ppermute x3, waiting for transfers between devices, per_device(): lax.ppermute(packed, 'blk', shift_pairs(count, step))  1.88 us
    pallas_call x1, Pallas kernels, per_device(): pl.pallas_call(functools.partial(stage_kernel, count=count, plan=plan, ro...  1.64 us
    pallas_call x2, Pallas kernels, per_device(): pl.pallas_call(functools.partial(next_kernel, start=start, scaling=scalin...  1 us
    pallas_call x1, Pallas kernels, per_device(): pl.pallas_call(functools.partial(pack_kernel, tiles=tiles), out_shape=jax...  0.89 us
    pallas_call x3, Pallas kernels, per_device(): pl.pallas_call(functools.partial(settle_kernel, messages=len(steps), firs...  0.83 us
  transfers between devices with their start and end apart: 6, of which 5 were waited for; matrix products, arithmetic and copies ran while one was open for 0% of the time, Pallas kernels for 12%

profile of v4, /device:TPU:0, one launch (start us, length us, event | category | flops | bytes accessed | tf_op | source)
XLA Modules:
  0.0 22.9 jit_solution(10954986876892884841)
XLA Ops:
  0.7 0.9 %shard_map.65.refs_4_ = bf16[272,128]{1,0:T(8,128)(2,1)S(1)} custom-call(s32[1]{0:T(128)S(6)} %copy.7.lengths_ref, s32[1,8]{1,0:T(1,128)} %positions_ref.1, bf16[1,8,32,128]{3,2,1,0:T(8,128)(2,1)} %queries_ref.1), custom_call_target="tpu_custom_call" | custom-call | tf_op jit(solution)/shard_map/pallas_call | solution.py:310
  1.6 3.1 %collective-permute-start.2 = (bf16[272,128]{1,0:T(8,128)(2,1)S(1)}, bf16[272,128]{1,0:T(8,128)(2,1)S(1)}, u32[]{:S(2)}, u32[]{:S(2)}) collective-permute-start(bf16[272,128]{1,0:T(8,128)(2,1)S(1)} %shard_map.65.refs_4_), channel_id=1, source_target_pairs={{0,4},{4,8},{8,12},{12,0},{1,5},{5,9},{9,13},{13,1},{2,6},{6,10},{... | collective-permute-start | bytes 208904 | tf_op jit(solution)/shard_map/ppermute | solution.py:322
  4.6 2.6 %collective-permute-start.1 = (bf16[272,128]{1,0:T(8,128)(2,1)S(1)}, bf16[272,128]{1,0:T(8,128)(2,1)S(1)}, u32[]{:S(2)}, u32[]{:S(2)}) collective-permute-start(bf16[272,128]{1,0:T(8,128)(2,1)S(1)} %shard_map.65.refs_4_), channel_id=1, source_target_pairs={{0,8},{4,12},{8,0},{12,4},{1,9},{5,13},{9,1},{13,5},{2,10},{6,14},... | collective-permute-start | bytes 208904 | tf_op jit(solution)/shard_map/ppermute | solution.py:322
  7.2 1.3 %collective-permute-start = (bf16[272,128]{1,0:T(8,128)(2,1)S(1)}, bf16[272,128]{1,0:T(8,128)(2,1)S(1)}, u32[]{:S(2)}, u32[]{:S(2)}) collective-permute-start(bf16[272,128]{1,0:T(8,128)(2,1)S(1)} %shard_map.65.refs_4_), channel_id=1, source_target_pairs={{0,12},{4,0},{8,4},{12,8},{1,13},{5,1},{9,5},{13,9},{2,14},{6,2},{... | collective-permute-start | bytes 208904 | tf_op jit(solution)/shard_map/ppermute | solution.py:322
  8.6 1.6 %shard_map.64 = (bf16[2,1024,128]{2,1,0:T(8,128)(2,1)S(1)}, bf16[2,128,1024]{2,1,0:T(8,128)(2,1)S(1)}, s32[1,32]{1,0:T(1,128)S(4)}, bf16[128,512]{1,0:T(8,128)(2,1)S(1)}) custom-call(bf16[1,2,1024,128]{3,2,1,0:T(8,128)(2,1)} %refs_0_.1, bf16[1,2,1024,128]{3,2,1,0:T(8,128)(2,1)} %refs_1_.1, s32[1,32]{1,0:T(1,128)} %refs_2_.1), custom_call_target="tpu_custom_call" | custom-call | flops 16777216 | bytes 1 | tf_op jit(solution)/shard_map/pallas_call | solution.py:327
  10.2 0.0 collective-permute-done.2.refs_7_
  10.2 1.7 %collective-permute-done.1.refs_6_ = bf16[272,128]{1,0:T(8,128)(2,1)S(1)} collective-permute-done((bf16[272,128]{1,0:T(8,128)(2,1)S(1)}, bf16[272,128]{1,0:T(8,128)(2,1)S(1)}, u32[]{:S(2)}, u32[]{:S(2)}) %collective-permute-start.1) | collective-permute-done | bytes 69664 | tf_op jit(solution)/shard_map/ppermute | solution.py:322
  11.9 0.2 collective-permute-done.refs_5_
  12.1 0.6 %shard_map.66 = (bf16[2,512,128]{2,1,0:T(8,128)(2,1)S(1)}, s32[8,512]{1,0:T(8,128)S(1)}, s16[272,128]{1,0:T(8,128)(2,1)S(1)}) custom-call(s32[1]{0:T(128)S(6)} %copy.7.lengths_ref, s32[1,32]{1,0:T(1,128)S(4)} %get-tuple-element.20.refs_0_, bf16[2,1024,128]{2,1,0:T(8,128)(2,1)S(1)} %get-tuple-element.18.refs_1_.refs_0_, ...), custom_call_target="tpu_custom_call" | custom-call | flops 1 | bytes 1 | tf_op jit(solution)/shard_map/pallas_call | solution.py:355
  12.7 0.9 %collective-permute-start.5 = (s16[272,128]{1,0:T(8,128)(2,1)S(1)}, s16[272,128]{1,0:T(8,128)(2,1)S(1)}, u32[]{:S(2)}, u32[]{:S(2)}) collective-permute-start(s16[272,128]{1,0:T(8,128)(2,1)S(1)} %get-tuple-element.26), channel_id=1, source_target_pairs={{0,8},{4,12},{8,0},{12,4},{1,9},{5,13},{9,1},{13,5},{2,10},{6,14},... | collective-permute-start | bytes 208904 | tf_op jit(solution)/shard_map/ppermute | solution.py:386
  13.5 0.5 %shard_map.67 = (s16[272,128]{1,0:T(8,128)(2,1)S(1)}, s16[272,128]{1,0:T(8,128)(2,1)S(1)}) custom-call(s32[1]{0:T(128)S(6)} %copy.7.lengths_ref, bf16[2,1024,128]{2,1,0:T(8,128)(2,1)S(1)} %get-tuple-element.18.refs_1_.refs_0_, bf16[2,128,1024]{2,1,0:T(8,128)(2,1)S(1)} %get-tuple-element.19.refs_2_.refs_1_, ...), custom_call_target="tpu_custom_call" | custom-call | flops 1 | bytes 1 | tf_op jit(solution)/shard_map/pallas_call | solution.py:375
  14.1 3.7 %collective-permute-start.4 = (s16[272,128]{1,0:T(8,128)(2,1)S(1)}, s16[272,128]{1,0:T(8,128)(2,1)S(1)}, u32[]{:S(2)}, u32[]{:S(2)}) collective-permute-start(s16[272,128]{1,0:T(8,128)(2,1)S(1)} %get-tuple-element.25), channel_id=1, source_target_pairs={{0,4},{4,8},{8,12},{12,0},{1,5},{5,9},{9,13},{13,1},{2,6},{6,10},{... | collective-permute-start | bytes 208904 | tf_op jit(solution)/shard_map/ppermute | solution.py:386
  17.8 0.5 %collective-permute-start.3 = (s16[272,128]{1,0:T(8,128)(2,1)S(1)}, s16[272,128]{1,0:T(8,128)(2,1)S(1)}, u32[]{:S(2)}, u32[]{:S(2)}) collective-permute-start(s16[272,128]{1,0:T(8,128)(2,1)S(1)} %get-tuple-element.24), channel_id=1, source_target_pairs={{0,12},{4,0},{8,4},{12,8},{1,13},{5,1},{9,5},{13,9},{2,14},{6,2},{... | collective-permute-start | bytes 208904 | tf_op jit(solution)/shard_map/ppermute | solution.py:386
  18.3 0.4 %shard_map.68.refs_0_ = s16[272,128]{1,0:T(8,128)(2,1)S(1)} custom-call(s32[1]{0:T(128)S(6)} %copy.7.lengths_ref, bf16[2,1024,128]{2,1,0:T(8,128)(2,1)S(1)} %get-tuple-element.18.refs_1_.refs_0_, bf16[2,128,1024]{2,1,0:T(8,128)(2,1)S(1)} %get-tuple-element.19.refs_2_.refs_1_, bf16[2,512,128]{2,1,0:T(8,128)(2,1)S(1)} %get-tuple-element.22.refs_2_, ...), custom_call_target="tpu_custom_call" | custom-call | flops 1 | bytes 1 | tf_op jit(solution)/shard_map/pallas_call | solution.py:375
  18.7 1.6 %collective-permute-done.5.refs_1_ = s16[272,128]{1,0:T(8,128)(2,1)S(1)} collective-permute-done((s16[272,128]{1,0:T(8,128)(2,1)S(1)}, s16[272,128]{1,0:T(8,128)(2,1)S(1)}, u32[]{:S(2)}, u32[]{:S(2)}) %collective-permute-start.5) | collective-permute-done | bytes 69664 | tf_op jit(solution)/shard_map/ppermute | solution.py:386
  20.4 1.1 %collective-permute-done.4.refs_0_ = s16[272,128]{1,0:T(8,128)(2,1)S(1)} collective-permute-done((s16[272,128]{1,0:T(8,128)(2,1)S(1)}, s16[272,128]{1,0:T(8,128)(2,1)S(1)}, u32[]{:S(2)}, u32[]{:S(2)}) %collective-permute-start.4) | collective-permute-done | bytes 69664 | tf_op jit(solution)/shard_map/ppermute | solution.py:386
  21.5 0.6 %collective-permute-done.3.refs_0_ = s16[272,128]{1,0:T(8,128)(2,1)S(1)} collective-permute-done((s16[272,128]{1,0:T(8,128)(2,1)S(1)}, s16[272,128]{1,0:T(8,128)(2,1)S(1)}, u32[]{:S(2)}, u32[]{:S(2)}) %collective-permute-start.3) | collective-permute-done | bytes 69664 | tf_op jit(solution)/shard_map/ppermute | solution.py:386
  22.2 0.8 %shard_map.71 = bf16[1,8,32,128]{3,2,1,0:T(8,128)(2,1)} custom-call(s16[272,128]{1,0:T(8,128)(2,1)S(1)} %collective-permute-done.3.refs_0_, f32[2,128,128]{2,1,0:T(8,128)S(1)} %get-tuple-element.29.refs_1_, f32[2,8,128]{2,1,0:T(8,128)S(1)} %get-tuple-element.30.refs_2_), custom_call_target="tpu_custom_call" | custom-call | flops 1 | bytes 1 | tf_op jit(solution)/shard_map/pallas_call | solution.py:400
  (2 shorter events, 0.1 us)
Async XLA Ops:
  1.6 8.7 %collective-permute-start.2 = (bf16[272,128]{1,0:T(8,128)(2,1)S(1)}, bf16[272,128]{1,0:T(8,128)(2,1)S(1)}, u32[]{:S(2)}, u32[]{:S(2)}) collective-permute-start(bf16[272,128]{1,0:T(8,128)(2,1)S(1)} %shard_map.65.refs_4_), channel_id=1, source_target_pairs={{0,4},{4,8},{8,12},{12,0},{1,5},{5,9},{9,13},{13,1},{2,6},{6,10},{... | collective-permute-start | bytes 208904 | tf_op jit(solution)/shard_map/ppermute | solution.py:322
  4.6 7.3 %collective-permute-start.1 = (bf16[272,128]{1,0:T(8,128)(2,1)S(1)}, bf16[272,128]{1,0:T(8,128)(2,1)S(1)}, u32[]{:S(2)}, u32[]{:S(2)}) collective-permute-start(bf16[272,128]{1,0:T(8,128)(2,1)S(1)} %shard_map.65.refs_4_), channel_id=1, source_target_pairs={{0,8},{4,12},{8,0},{12,4},{1,9},{5,13},{9,1},{13,5},{2,10},{6,14},... | collective-permute-start | bytes 208904 | tf_op jit(solution)/shard_map/ppermute | solution.py:322
  7.2 4.9 %collective-permute-start = (bf16[272,128]{1,0:T(8,128)(2,1)S(1)}, bf16[272,128]{1,0:T(8,128)(2,1)S(1)}, u32[]{:S(2)}, u32[]{:S(2)}) collective-permute-start(bf16[272,128]{1,0:T(8,128)(2,1)S(1)} %shard_map.65.refs_4_), channel_id=1, source_target_pairs={{0,12},{4,0},{8,4},{12,8},{1,13},{5,1},{9,5},{13,9},{2,14},{6,2},{... | collective-permute-start | bytes 208904 | tf_op jit(solution)/shard_map/ppermute | solution.py:322
  12.7 7.7 %collective-permute-start.5 = (s16[272,128]{1,0:T(8,128)(2,1)S(1)}, s16[272,128]{1,0:T(8,128)(2,1)S(1)}, u32[]{:S(2)}, u32[]{:S(2)}) collective-permute-start(s16[272,128]{1,0:T(8,128)(2,1)S(1)} %get-tuple-element.26), channel_id=1, source_target_pairs={{0,8},{4,12},{8,0},{12,4},{1,9},{5,13},{9,1},{13,5},{2,10},{6,14},... | collective-permute-start | bytes 208904 | tf_op jit(solution)/shard_map/ppermute | solution.py:386
  14.1 7.4 %collective-permute-start.4 = (s16[272,128]{1,0:T(8,128)(2,1)S(1)}, s16[272,128]{1,0:T(8,128)(2,1)S(1)}, u32[]{:S(2)}, u32[]{:S(2)}) collective-permute-start(s16[272,128]{1,0:T(8,128)(2,1)S(1)} %get-tuple-element.25), channel_id=1, source_target_pairs={{0,4},{4,8},{8,12},{12,0},{1,5},{5,9},{9,13},{13,1},{2,6},{6,10},{... | collective-permute-start | bytes 208904 | tf_op jit(solution)/shard_map/ppermute | solution.py:386
  17.8 4.4 %collective-permute-start.3 = (s16[272,128]{1,0:T(8,128)(2,1)S(1)}, s16[272,128]{1,0:T(8,128)(2,1)S(1)}, u32[]{:S(2)}, u32[]{:S(2)}) collective-permute-start(s16[272,128]{1,0:T(8,128)(2,1)S(1)} %get-tuple-element.24), channel_id=1, source_target_pairs={{0,12},{4,0},{8,4},{12,8},{1,13},{5,1},{9,5},{13,9},{2,14},{6,2},{... | collective-permute-start | bytes 208904 | tf_op jit(solution)/shard_map/ppermute | solution.py:386
